TPU v7x, 512 devices: a whole 4x4x16 slice. The times are simulated.
512 devices in a mesh: pipe: 32 (over z, x_lo), dp: 16 (over y, x_hi, core).
Axes of the slice: x: 4 (x_hi: 2, x_lo: 2; x = x_hi * 2 + x_lo), y: 4, z: 16, core: 2. Of those that a mesh axis runs over, the one named last changes fastest.
Arguments:
- fwd_in: bfloat16 [32, 2, 256, 7168], P('pipe', None, None, 'dp'), may hold values from -6 to 6
- stash: bfloat16 [32, 2, 256, 7168], P('pipe', None, None, 'dp'), may hold values from -6 to 6
- cot_in: bfloat16 [32, 2, 256, 7168], P('pipe', None, None, 'dp'), may hold values from -6 to 6
- w_down: bfloat16 [32, 2, 7168, 512], P('pipe', None, 'dp'), may hold values from -0.04783613 to 0.04783613, as said below
- w_up: bfloat16 [32, 2, 512, 7168], P('pipe', None, None, 'dp'), may hold values from -0.1789864 to 0.1789864, as said below
- gain: float32 [32, 2, 7168], P('pipe', None, 'dp'), may hold values from 0.5 to 2, as said below
Outputs:
- fwd_next: bfloat16 [32, 2, 256, 7168], P('pipe', None, None, 'dp')
- bwd_next: bfloat16 [32, 2, 256, 7168], P('pipe', None, None, 'dp')
- grad_down: bfloat16 [32, 7168, 512], P('pipe', 'dp')
- grad_up: bfloat16 [32, 512, 7168], P('pipe', None, 'dp')
- grad_gain: bfloat16 [32, 7168], P('pipe', 'dp')
Inputs may be any that keep to these rules, and one draw needn't show every extreme that they name: w_down[s, 1] equals w_down[31 - s, 0] for every position s: both slots hold copies of sections. w_up[s, 1] equals w_up[31 - s, 0] for every position s. gain[s, 1] equals gain[31 - s, 0] for every position s.
All inputs are finite; a program needn't handle non-finite values.
Results may differ from a plain program's by a relative error of at most 0.02.
Values may be sent and summed in bfloat16 or wider, within the bound.
A program may use at most 64 MiB of HBM per device.

v0:
```python
import math

import jax
import jax.numpy as jnp
from jax import lax
from jax.sharding import PartitionSpec as P

EPS = 1e-06


def shifted(block, axis, distance):
    devices = range(lax.axis_size(axis))
    route = [(i - distance, i) for i in devices if i - distance in devices]
    return lax.ppermute(block, axis, route)


def from_partner(block, axis, distance):
    count = lax.axis_size(axis)
    route = []
    for low in range(count):
        high = low | 1 << distance
        if high != low and high < count:
            route += [(low, high), (high, low)]
    return lax.ppermute(block, axis, route)


def row_total(partial_rows):
    return lax.psum(partial_rows, "dp")


def row_norm(rows):
    wide = rows.astype(jnp.float32)
    features = rows.shape[-1] * lax.axis_size("dp")
    squares = row_total(jnp.sum(wide * wide, axis=-1, keepdims=True))
    inverse = lax.rsqrt(squares / features + EPS)
    return (wide, inverse, (wide * inverse).astype(jnp.bfloat16))


def neighbors(values, offset):
    return shifted(values, "pipe", offset)


def sum_latent(partial_sums):
    totals = lax.psum(partial_sums, "dp")
    return totals


def unit_latent(latent):
    inverse = lax.rsqrt(jnp.mean(latent * latent, axis=-1, keepdims=True) + EPS)
    return (inverse, latent * inverse)


def forward_span(inputs, weights_down, weights_up, gain_cols):
    wide, inverse, normed = row_norm(inputs)
    scaled = (normed.astype(jnp.float32) * gain_cols[:, None, :]).astype(jnp.bfloat16)
    latent = sum_latent(
        jnp.einsum("ktd,kdr->ktr", scaled, weights_down, preferred_element_type=jnp.float32)
    )
    lat_inverse, lat_unit = unit_latent(latent)
    lat_rows = lat_unit.astype(jnp.bfloat16)
    branch = jnp.einsum(
        "ktr,krd->ktd", lat_rows, weights_up, preferred_element_type=jnp.float32
    ).astype(jnp.bfloat16)
    return (wide + branch.astype(jnp.float32)).astype(jnp.bfloat16)


def backward_span(stored, cotangent, weights_down, weights_up, gain_cols):
    wide, inverse, normed = row_norm(stored)
    features = stored.shape[-1] * lax.axis_size("dp")
    scaled = (normed.astype(jnp.float32) * gain_cols[:, None, :]).astype(jnp.bfloat16)
    latent_part = jnp.einsum(
        "ktd,kdr->ktr", scaled, weights_down, preferred_element_type=jnp.float32
    )
    lat_cot_part = jnp.einsum(
        "ktd,krd->ktr", cotangent, weights_up, preferred_element_type=jnp.float32
    )
    sums = sum_latent(jnp.concatenate([latent_part, lat_cot_part], axis=0))
    latent = sums[:2]
    lat_cot = sums[2:]
    lat_inverse, lat_unit = unit_latent(latent)
    latent_cot = lat_inverse * (
        lat_cot - lat_unit * jnp.mean(lat_cot * lat_unit, axis=-1, keepdims=True)
    )
    spread = jnp.concatenate(
        [lat_unit.astype(jnp.bfloat16), latent_cot.astype(jnp.bfloat16)], axis=0
    )
    lat_rows = spread[:2]
    cot_rows = spread[2:]
    up_grad = jnp.einsum("ktr,ktd->krd", lat_rows, cotangent, preferred_element_type=jnp.float32)
    down_grad = jnp.einsum("ktd,ktr->kdr", scaled, cot_rows, preferred_element_type=jnp.float32)
    scaled_cot = jnp.einsum(
        "ktr,kdr->ktd", cot_rows, weights_down, preferred_element_type=jnp.float32
    )
    gain_grad = jnp.sum(normed.astype(jnp.float32) * scaled_cot, axis=1)
    cot_wide = (scaled_cot * gain_cols[:, None, :]).astype(jnp.bfloat16).astype(jnp.float32)
    unit_rows = wide * inverse
    projection = row_total(jnp.sum(cot_wide * unit_rows, axis=-1, keepdims=True)) / features
    input_cot = cotangent.astype(jnp.float32) + inverse * (cot_wide - unit_rows * projection)
    return (input_cot.astype(jnp.bfloat16), down_grad, up_grad, gain_grad)


def per_device(fwd_in, stash, cot_in, w_down, w_up, gain):
    weights_down = w_down[0]
    weights_up = w_up[0]
    gain_cols = gain[0]
    outputs = forward_span(fwd_in[0], weights_down, weights_up, gain_cols)
    from_below = neighbors(outputs[0], 1)
    from_above = neighbors(outputs[1], -1)
    input_cot, down_grad, up_grad, gain_grad = backward_span(
        stash[0], cot_in[0], weights_down, weights_up, gain_cols
    )
    cot_above = neighbors(input_cot[0], -1)
    cot_below = neighbors(input_cot[1], 1)
    fwd_next = jnp.stack([from_below, from_above])[None]
    bwd_next = jnp.stack([cot_above, cot_below])[None]
    factor = 1.0 / math.sqrt(fwd_in.shape[2])
    copy_down = (down_grad * factor).astype(jnp.bfloat16)
    copy_up = (up_grad * factor).astype(jnp.bfloat16)
    copy_gain = (gain_grad * factor).astype(jnp.bfloat16)
    size_down = copy_down.shape[1] * copy_down.shape[2]
    size_up = copy_up.shape[1] * copy_up.shape[2]
    flat = jnp.concatenate([copy_down[1].reshape(-1), copy_up[1].reshape(-1), copy_gain[1]])
    for bit_index in range(lax.axis_size("pipe").bit_length() - 1):
        flat = from_partner(flat, "pipe", bit_index)
    mirror_down = flat[:size_down].reshape(copy_down.shape[1:])
    mirror_up = flat[size_down : size_down + size_up].reshape(copy_up.shape[1:])
    mirror_gain = flat[size_down + size_up :]
    grad_down = (copy_down[0].astype(jnp.float32) + mirror_down.astype(jnp.float32)).astype(
        jnp.bfloat16
    )[None]
    grad_up = (copy_up[0].astype(jnp.float32) + mirror_up.astype(jnp.float32)).astype(jnp.bfloat16)[
        None
    ]
    grad_gain = (copy_gain[0].astype(jnp.float32) + mirror_gain.astype(jnp.float32)).astype(
        jnp.bfloat16
    )[None]
    return (fwd_next, bwd_next, grad_down, grad_up, grad_gain)


def solution(mesh):
    placed = (
        P("pipe", None, None, "dp"),
        P("pipe", None, None, "dp"),
        P("pipe", None, None, "dp"),
        P("pipe", None, "dp", None),
        P("pipe", None, None, "dp"),
        P("pipe", None, "dp"),
    )
    return jax.shard_map(
        per_device,
        mesh=mesh,
        in_specs=placed,
        out_specs=(
            P("pipe", None, None, "dp"),
            P("pipe", None, None, "dp"),
            P("pipe", "dp", None),
            P("pipe", None, "dp"),
            P("pipe", "dp"),
        ),
        check_vma=False,
    )
```

profile of v0, /device:TPU:3, one launch (start us, length us, event | category | flops | bytes accessed | tf_op | source)
XLA Modules:
  0.0 581.6 jit_solution(1310721028153653569)
XLA Ops:
  7.2 1.2 fusion.11
  8.5 33.2 %psum.37 = f32[2,256,1]{1,0,2:T(2,128)S(1)} all-reduce(f32[2,256,1]{1,0,2:T(2,128)S(1)} %bitcast.82), channel_id=1, replica_groups=mesh['pipe'=32,'dp'=16] {'dp'}, use_global_device_ids=true, to_apply=%region_5.0 | all-reduce | flops 512 | bytes 4096 | tf_op jit(solution)/shard_map/psum | solution.py:28
  41.7 1.8 fusion.14
  43.5 0.7 fusion.19
  44.3 1.5 pad_maximum_fusion
  45.8 0.0 all-reduce.4.cloned.1.call-start
  45.8 164.4 %all-reduce.6.cloned.1.call-done = f32[4,256,512]{2,1,0:T(8,128)} async-done(((f32[4,256,512]{2,1,0:T(8,128)}), f32[4,256,512]{2,1,0:T(8,128)}) %all-reduce.6.cloned.1.call-update) | async-done | bytes 2097168 | tf_op jit(solution)/shard_map/psum | solution.py:44
  210.2 1.5 multiply_reduce_fusion.1
  211.7 1.8 multiply_reduce_fusion
  213.5 0.2 multiply_convert_fusion.2
  213.8 1.4 multiply_convert_fusion.1
  215.2 1.5 fusion.6
  216.7 0.5 multiply_convert_fusion
  217.2 1.0 copy.11
  218.2 2.4 reshape_squeeze.7
  220.6 1.1 slice_bitcast_fusion
  221.7 0.2 copy.13
  221.9 0.1 pad_maximum_fusion.1
  222.0 3.1 collective-permute-start.4
  225.1 18.9 %collective-permute-done.4 = bf16[459200]{0:T(1024)(128)(2,1)S(1)} collective-permute-done((bf16[459200]{0:T(1024)(128)(2,1)S(1)}, bf16[459200]{0:T(1024)(128)(2,1)S(1)}, u32[]{:S(2)}, u32[]{:S(2)}) %collective-permute-start.4) | collective-permute-done | bytes 918432 | tf_op jit(solution)/shard_map/ppermute | solution.py:24
  244.0 3.1 collective-permute-start.5
  247.2 18.0 %collective-permute-done.5 = bf16[459200]{0:T(1024)(128)(2,1)} collective-permute-done((bf16[459200]{0:T(1024)(128)(2,1)S(1)}, bf16[459200]{0:T(1024)(128)(2,1)}, u32[]{:S(2)}, u32[]{:S(2)}) %collective-permute-start.5) | collective-permute-done | bytes 918432 | tf_op jit(solution)/shard_map/ppermute | solution.py:24
  265.2 4.1 collective-permute-start.6
  269.3 0.1 fusion.12
  269.5 36.4 %all-reduce = (f32[2,256,1]{1,0,2:T(2,128)S(1)}, f32[2,256,1]{1,0,2:T(2,128)S(1)}) all-reduce(f32[2,256,1]{1,0,2:T(2,128)S(1)} %bitcast.81, f32[2,256,1]{1,0,2:T(2,128)S(1)} %bitcast.84), channel_id=1, replica_groups=mesh['pipe'=32,'dp'=16] {'dp'}, use_global_device_ids=true, to_apply=%region_1.0 | all-reduce | flops 1024 | bytes 8192 | tf_op jit(solution)/shard_map/psum | solution.py:28
  305.9 1.8 fusion.21
  307.7 1.6 collective-permute-done.6
  309.3 7.3 %collective-permute-start.7 = (bf16[459200]{0:T(1024)(128)(2,1)}, bf16[459200]{0:T(1024)(128)(2,1)}, u32[]{:S(2)}, u32[]{:S(2)}) collective-permute-start(bf16[459200]{0:T(1024)(128)(2,1)} %collective-permute-done.6), channel_id=1, source_target_pairs={{0,128},{128,0},{16,144},{144,16},{32,160},{160,32},{48,176},{176,... | collective-permute-start | bytes 2755208 | tf_op jit(solution)/shard_map/ppermute | solution.py:24
  316.6 1.5 fusion.9
  318.1 3.2 collective-permute-start.2
  321.3 3.0 collective-permute-start.3
  324.3 141.6 %all-reduce.4.cloned.1.call-done = f32[2,256,512]{2,1,0:T(8,128)} async-done(((f32[2,256,512]{2,1,0:T(8,128)}), f32[2,256,512]{2,1,0:T(8,128)}) %all-reduce.4.cloned.1.call-update) | async-done | bytes 1048592 | tf_op jit(solution)/shard_map/psum | solution.py:44
  465.9 1.4 multiply_reduce_fusion.2
  467.3 12.5 %collective-permute-start.8 = (bf16[459200]{0:T(1024)(128)(2,1)}, bf16[459200]{0:T(1024)(128)(2,1)S(1)}, u32[]{:S(2)}, u32[]{:S(2)}) collective-permute-start(bf16[459200]{0:T(1024)(128)(2,1)} %collective-permute-done.7), channel_id=1, source_target_pairs={{0,256},{256,0},{16,272},{272,16},{32,288},{288,32},{48,304},{304,... | collective-permute-start | bytes 2755208 | tf_op jit(solution)/shard_map/ppermute | solution.py:24
  479.9 2.0 fusion.1
  481.9 3.2 collective-permute-start
  485.1 2.1 collective-permute-start.1
  487.2 1.8 maximum_bitcast_fusion.1
  489.0 73.5 %collective-permute-done = bf16[256,448]{0,1:T(8,128)(2,1)S(1)} collective-permute-done((bf16[256,448]{0,1:T(8,128)(2,1)S(1)}, bf16[256,448]{0,1:T(8,128)(2,1)S(1)}, u32[]{:S(2)}, u32[]{:S(2)}) %collective-permute-start) | collective-permute-done | bytes 229408 | tf_op jit(solution)/shard_map/ppermute | solution.py:14
  562.5 2.5 collective-permute-done.1
  565.0 0.8 maximum_bitcast_fusion
  565.8 0.6 broadcast_in_dim.28
  566.4 1.4 slice_convert_fusion
  567.7 1.5 reshape.70
  569.2 1.3 copy.12
  570.5 2.2 add_convert_fusion
  572.7 0.1 reshape.69
  572.9 1.9 add_convert_fusion.1
  (35 shorter events, 0.3 us)
Async XLA Ops:
  7.2 36.3 %copy-start = (bf16[1,2,448,512]{3,2,1,0:T(8,128)(2,1)S(1)}, bf16[1,2,448,512]{3,2,1,0:T(8,128)(2,1)}, u32[]{:S(2)}) copy-start(bf16[1,2,448,512]{3,2,1,0:T(8,128)(2,1)} %param.9) | copy-start | bytes 2752516
  7.2 36.3 %copy-start.4 = (bf16[1,2,256,448]{2,3,1,0:T(8,128)(2,1)S(1)}, bf16[1,2,256,448]{2,3,1,0:T(8,128)(2,1)}, u32[]{:S(2)}) copy-start(bf16[1,2,256,448]{2,3,1,0:T(8,128)(2,1)} %param.7) | copy-start | bytes 1376260
  7.2 36.3 %copy-start.7 = (f32[1,2,448]{2,1,0:T(2,128)S(1)}, f32[1,2,448]{2,1,0:T(2,128)}, u32[]{:S(2)}) copy-start(f32[1,2,448]{2,1,0:T(2,128)} %param.11) | copy-start | bytes 10756
  7.2 203.0 %all-reduce.6.cloned.1.call-start = ((), (), s32[]{:S(2)}) async-start(), calls=%async_computation.1 | async-start | bytes 4194304 | tf_op jit(solution)/shard_map/psum | solution.py:44
  45.8 420.2 %all-reduce.4.cloned.1.call-start = ((), (), s32[]{:S(2)}) async-start(), calls=%async_computation | async-start | bytes 2097152 | tf_op jit(solution)/shard_map/psum | solution.py:44
  210.2 3.4 copy-start.1
  215.2 1.5 copy-start.3
  220.6 1.4 copy-start.6
  220.6 48.7 %copy-start.2 = (bf16[1,2,256,448]{2,3,1,0:T(8,128)(2,1)S(1)}, bf16[1,2,256,448]{2,3,1,0:T(8,128)(2,1)}, u32[]{:S(2)}) copy-start(bf16[1,2,256,448]{2,3,1,0:T(8,128)(2,1)} %param.6) | copy-start | bytes 1376260
  222.0 22.0 %collective-permute-start.4 = (bf16[459200]{0:T(1024)(128)(2,1)S(1)}, bf16[459200]{0:T(1024)(128)(2,1)S(1)}, u32[]{:S(2)}, u32[]{:S(2)}) collective-permute-start(bf16[459200]{0:T(1024)(128)(2,1)S(1)} %pad_maximum_fusion.1), channel_id=1, source_target_pairs={{0,16},{16,0},{32,48},{48,32},{64,80},{80,64},{96,112},{112,96},{1... | collective-permute-start | bytes 2755208 | tf_op jit(solution)/shard_map/ppermute | solution.py:24
  244.0 21.2 %collective-permute-start.5 = (bf16[459200]{0:T(1024)(128)(2,1)S(1)}, bf16[459200]{0:T(1024)(128)(2,1)}, u32[]{:S(2)}, u32[]{:S(2)}) collective-permute-start(bf16[459200]{0:T(1024)(128)(2,1)S(1)} %collective-permute-done.4), channel_id=1, source_target_pairs={{0,32},{32,0},{16,48},{48,16},{64,96},{96,64},{80,112},{112,80},{1... | collective-permute-start | bytes 2755208 | tf_op jit(solution)/shard_map/ppermute | solution.py:24
  265.2 44.1 %collective-permute-start.6 = (bf16[459200]{0:T(1024)(128)(2,1)}, bf16[459200]{0:T(1024)(128)(2,1)}, u32[]{:S(2)}, u32[]{:S(2)}) collective-permute-start(bf16[459200]{0:T(1024)(128)(2,1)} %collective-permute-done.5), channel_id=1, source_target_pairs={{0,64},{64,0},{16,80},{80,16},{32,96},{96,32},{48,112},{112,48},{1... | collective-permute-start | bytes 2755208 | tf_op jit(solution)/shard_map/ppermute | solution.py:24
  309.3 158.0 %collective-permute-start.7 = (bf16[459200]{0:T(1024)(128)(2,1)}, bf16[459200]{0:T(1024)(128)(2,1)}, u32[]{:S(2)}, u32[]{:S(2)}) collective-permute-start(bf16[459200]{0:T(1024)(128)(2,1)} %collective-permute-done.6), channel_id=1, source_target_pairs={{0,128},{128,0},{16,144},{144,16},{32,160},{160,32},{48,176},{176,... | collective-permute-start | bytes 2755208 | tf_op jit(solution)/shard_map/ppermute | solution.py:24
  318.1 169.1 %collective-permute-start.2 = (bf16[256,448]{0,1:T(8,128)(2,1)S(1)}, bf16[256,448]{0,1:T(8,128)(2,1)S(1)}, u32[]{:S(2)}, u32[]{:S(2)}) collective-permute-start(bf16[256,448]{0,1:T(8,128)(2,1)S(1)} %get-tuple-element.11), channel_id=1, source_target_pairs={{16,0},{32,16},{48,32},{64,48},{80,64},{96,80},{112,96},{128,112},... | collective-permute-start | bytes 688136 | tf_op jit(solution)/shard_map/ppermute | solution.py:14
  321.3 166.0 %collective-permute-start.3 = (bf16[256,448]{0,1:T(8,128)(2,1)S(1)}, bf16[256,448]{0,1:T(8,128)(2,1)}, u32[]{:S(2)}, u32[]{:S(2)}) collective-permute-start(bf16[256,448]{0,1:T(8,128)(2,1)S(1)} %get-tuple-element.12), channel_id=1, source_target_pairs={{0,16},{16,32},{32,48},{48,64},{64,80},{80,96},{96,112},{112,128},... | collective-permute-start | bytes 688136 | tf_op jit(solution)/shard_map/ppermute | solution.py:14
  467.3 98.5 %collective-permute-start.8 = (bf16[459200]{0:T(1024)(128)(2,1)}, bf16[459200]{0:T(1024)(128)(2,1)S(1)}, u32[]{:S(2)}, u32[]{:S(2)}) collective-permute-start(bf16[459200]{0:T(1024)(128)(2,1)} %collective-permute-done.7), channel_id=1, source_target_pairs={{0,256},{256,0},{16,272},{272,16},{32,288},{288,32},{48,304},{304,... | collective-permute-start | bytes 2755208 | tf_op jit(solution)/shard_map/ppermute | solution.py:24
  481.9 80.6 %collective-permute-start = (bf16[256,448]{0,1:T(8,128)(2,1)S(1)}, bf16[256,448]{0,1:T(8,128)(2,1)S(1)}, u32[]{:S(2)}, u32[]{:S(2)}) collective-permute-start(bf16[256,448]{0,1:T(8,128)(2,1)S(1)} %get-tuple-element.13), channel_id=1, source_target_pairs={{0,16},{16,32},{32,48},{48,64},{64,80},{80,96},{96,112},{112,128},... | collective-permute-start | bytes 688136 | tf_op jit(solution)/shard_map/ppermute | solution.py:14
  485.1 79.9 %collective-permute-start.1 = (bf16[256,448]{0,1:T(8,128)(2,1)S(1)}, bf16[256,448]{0,1:T(8,128)(2,1)S(1)}, u32[]{:S(2)}, u32[]{:S(2)}) collective-permute-start(bf16[256,448]{0,1:T(8,128)(2,1)S(1)} %get-tuple-element.14), channel_id=1, source_target_pairs={{16,0},{32,16},{48,32},{64,48},{80,64},{96,80},{112,96},{128,112},... | collective-permute-start | bytes 688136 | tf_op jit(solution)/shard_map/ppermute | solution.py:14
  570.5 2.2 copy-start.5
Sparse Core Ops, SparseCore 0:
  45.9 164.2 all-reduce.5
  307.8 158.0 all-reduce.3
where the time goes:
time: 583 us; the launch traced here: 582 us
  waiting for transfers between devices  421 us (72%)
  blocking collectives  69.6 us (12%)
  starting transfers between devices  41.7 us (7%)
  other arithmetic  17.4 us (3%)
  between operations  14.3 us (2%)
  matrix products  9.72 us (2%)
  local copies, waits for them, and re-layouts  8.35 us (1%)
    psum x2, waiting for transfers between devices, sum_latent(): totals = lax.psum(partial_sums, 'dp')  306 us
    ppermute x4, waiting for transfers between devices, shifted(): return lax.ppermute(block, axis, route)  76 us
    psum x2, blocking collectives, row_total(): return lax.psum(partial_rows, 'dp')  69.6 us
    ppermute x5, waiting for transfers between devices, from_partner(): return lax.ppermute(block, axis, route)  38.6 us
    ppermute x5, starting transfers between devices, from_partner(): return lax.ppermute(block, axis, route)  30.2 us
  transfers between devices with their start and end apart: 11, of which 7 were waited for; matrix products, arithmetic and copies ran while one was open for 2% of the time, Pallas kernels for 0%

commit v1 on v0

v1 whole, which is shorter than its diff:
```python
import functools

import jax
import jax.numpy as jnp
from jax import lax
from jax.experimental import pallas as pl
from jax.experimental.pallas import tpu as pltpu
from jax.sharding import PartitionSpec as P

MESH = pl.DeviceIdType.MESH
EPS = 1e-06
BF16 = jnp.bfloat16
F32 = jnp.float32

Y, XH, CORE = 4, 2, 2


def dot(a, b, ca, cb):
    return lax.dot_general(a, b, (((ca,), (cb,)), ((), ())), preferred_element_type=F32)


def kernel(
    n_pipe,
    fwd_ref,
    stash_ref,
    cot_ref,
    wd_ref,
    wu_ref,
    gain_ref,
    fwd_out,
    bwd_out,
    gd_out,
    gu_out,
    gg_out,
    part,
    r1,
    r2,
    h2,
    r3,
    full,
    zg,
    tail,
    mz,
    md,
    mt,
    gsend,
    grecv,
    rows_out,
    down_acc,
    up_acc,
    core_s,
    core_r,
    y_s,
    y_r,
    x_s,
    x_r,
    gx_s,
    gx_r,
    gy_s,
    gy_r,
    gc_s,
    gc_r,
    m_s,
    m_r,
    n_s,
    n_r,
    zero_sem,
):
    pos = lax.axis_index("pipe")
    d = lax.axis_index("dp")
    tokens, cols = stash_ref.shape[1:]
    lat = wd_ref.shape[2]
    features = cols * Y * XH * CORE
    two = 2 * lat
    main = cols // 128 * 128
    rest = cols - main
    half, quarter, own = tokens // 2, tokens // 8, tokens // 16
    core = d % CORE
    xh = d // CORE % XH
    y = d // (CORE * XH)
    sibling = (pos, d + 1 - 2 * core)
    across = (pos, d + CORE * (1 - 2 * xh))
    ring = [(pos, (y + k) % Y * (CORE * XH) + d % (CORE * XH)) for k in range(1, Y)]
    mirror = (n_pipe - 1 - pos, d)
    above = ((pos + 1) % n_pipe, d)
    below = ((pos + n_pipe - 1) % n_pipe, d)

    def send(src, dst, s_sem, r_sem, device):
        return pltpu.make_async_remote_copy(
            src_ref=src,
            dst_ref=dst,
            send_sem=s_sem,
            recv_sem=r_sem,
            device_id=device,
            device_id_type=MESH,
        )

    barrier = pltpu.get_barrier_semaphore()
    partners = [sibling, across, *ring, mirror, above, below]
    for device in partners:
        pl.semaphore_signal(barrier, inc=1, device_id=device, device_id_type=MESH)
    pl.semaphore_wait(barrier, len(partners))

    mirror_dy = send(cot_ref.at[1, :, :main], md, m_s.at[0], m_r.at[0], mirror)
    mirror_dy.start()
    wide1 = stash_ref[1].astype(F32)
    scaled1 = wide1 * gain_ref[1:2, :]
    zg[1] = scaled1.astype(BF16)
    mirror_z = send(zg.at[1, :, :main], mz, m_s.at[1], m_r.at[1], mirror)
    mirror_z.start()
    tail[...] = jnp.concatenate(
        [cot_ref[1, :, main:].astype(F32), scaled1[:, main:]], axis=1
    ).astype(BF16)
    mirror_t = send(tail, mt, m_s.at[2], m_r.at[2], mirror)
    mirror_t.start()

    def squares(wide):
        return jnp.sum(wide * wide, axis=1, keepdims=True)

    core_copies = []

    def core_send(g):
        away = pl.multiple_of((1 - core) * half, half)
        copy = send(part.at[g, pl.ds(away, half), :], r1.at[g], core_s.at[g], core_r.at[g], sibling)
        copy.start()
        core_copies.append(copy)

    for g, slot in ((0, 1), (1, 0)):
        wide = stash_ref[slot].astype(F32)
        if slot == 0:
            zg[0] = (wide * gain_ref[0:1, :]).astype(BF16)
        part[g, :, :lat] = dot(zg[slot], wd_ref[slot], 1, 0).astype(BF16)
        part[g, :, lat:two] = dot(cot_ref[slot], wu_ref[slot], 1, 1).astype(BF16)
        part[g, :, two:] = jnp.broadcast_to(squares(wide), (tokens, 128)).astype(BF16)
        core_send(g)
    norms = []
    for slot in range(2):
        wide = fwd_ref[slot].astype(F32)
        norms.append(squares(wide))
        rows = (wide * gain_ref[slot : slot + 1, :]).astype(BF16)
        part[2, :, slot * lat : (slot + 1) * lat] = dot(rows, wd_ref[slot], 1, 0).astype(BF16)
    lane = lax.broadcasted_iota(jnp.int32, (tokens, 128), 1)
    part[2, :, two:] = jnp.where(lane < 64, norms[0], norms[1]).astype(BF16)
    core_send(2)

    ring_copies = []
    for g in range(3):
        core_copies[g].wait_recv()
        mine = part[g, pl.ds(pl.multiple_of(core * half, half), half), :].astype(F32)
        r1[g] = (mine + r1[g].astype(F32)).astype(BF16)
        for k in range(1, Y):
            to = pl.multiple_of((y + k) % Y * quarter, quarter)
            copy = send(
                r1.at[g, pl.ds(to, quarter), :],
                r2.at[g, k - 1],
                y_s.at[g, k - 1],
                y_r.at[g, k - 1],
                ring[k - 1],
            )
            copy.start()
            ring_copies.append(copy)
    x_copies = []
    for g in range(3):
        total = r1[g, pl.ds(pl.multiple_of(y * quarter, quarter), quarter), :].astype(F32)
        for k in range(Y - 1):
            ring_copies[g * 3 + k].wait_recv()
            total = total + r2[g, k].astype(F32)
        h2[g] = total.astype(BF16)
        copy = send(
            h2.at[g, pl.ds(pl.multiple_of((1 - xh) * own, own), own), :],
            r3.at[g],
            x_s.at[g],
            x_r.at[g],
            across,
        )
        copy.start()
        x_copies.append(copy)

    base = pl.multiple_of(core * half + y * quarter + xh * own, own)
    block = pl.multiple_of(core * half + y * quarter, quarter)

    def mean_sq(values):
        return jnp.sum(values * values, axis=1, keepdims=True) / lat

    mirror_rows = send(
        full.at[0, pl.ds(base, own), :two],
        full.at[3, pl.ds(base, own), :two],
        m_s.at[3],
        m_r.at[3],
        mirror,
    )
    gx_copies = {}
    widths = (two + 128, two + 128, two, two)

    def gx_send(g):
        spot = full.at[g, pl.ds(base, own), : widths[g]]
        gx_copies[g] = send(spot, spot, gx_s.at[g], gx_r.at[g], across)
        gx_copies[g].start()

    for g in range(3):
        x_copies[g].wait_recv()
        total = h2[g, pl.ds(pl.multiple_of(xh * own, own), own), :].astype(F32) + r3[g].astype(F32)
        first, second = total[:, :lat], total[:, lat:two]
        square = total[:, two : two + 1] / features + EPS
        scale = lax.rsqrt(mean_sq(first) + EPS * square)
        unit = first * scale
        full[g, pl.ds(base, own), :lat] = unit.astype(BF16)
        if g < 2:
            mean = jnp.sum(second * unit, axis=1, keepdims=True) / lat
            cot = (scale * (second - unit * mean)).astype(BF16)
            full[g, pl.ds(base, own), lat:two] = cot
            pull = jnp.sum(cot.astype(F32) * first, axis=1, keepdims=True) / (features * square)
            full[g, pl.ds(base, own), two:] = jnp.broadcast_to(pull, (own, 128)).astype(BF16)
        else:
            square = total[:, two + 64 : two + 65] / features + EPS
            scale = lax.rsqrt(mean_sq(second) + EPS * square)
            full[g, pl.ds(base, own), lat:two] = (second * scale).astype(BF16)
        if g == 0:
            mirror_rows.start()
        gx_send(g)

    gy_copies, gc_copies = {}, {}

    def gc_send(g, index, row):
        spot = full.at[g, pl.ds(row, quarter), : widths[g]]
        gc_copies[g, index] = send(spot, spot, gc_s.at[g, index], gc_r.at[g, index], sibling)
        gc_copies[g, index].start()

    def gy_send(g):
        gx_copies[g].wait_recv()
        spot = full.at[g, pl.ds(block, quarter), : widths[g]]
        for k in range(1, Y):
            gy_copies[g, k] = send(spot, spot, gy_s.at[g, k - 1], gy_r.at[g, k - 1], ring[k - 1])
            gy_copies[g, k].start()
        gc_send(g, 0, block)

    def gy_pass(g):
        for k in range(1, Y):
            gy_copies[g, k].wait_recv()
            row = pl.multiple_of(core * half + (y + Y - k) % Y * quarter, quarter)
            gc_send(g, k, row)

    def gc_wait(g):
        for k in range(Y):
            gc_copies[g, k].wait_recv()

    ups = (pos < n_pipe - 1, pos > 0)

    def relay(index, slot, out, up):
        return send(rows_out.at[index], out.at[slot], n_s.at[index], n_r.at[index], above if up else below)

    relays = [relay(0, 1, bwd_out, True), relay(1, 0, bwd_out, False), relay(2, 0, fwd_out, True), relay(3, 1, fwd_out, False)]

    def relay_start(index):
        @pl.when(ups[index % 2])
        def _():
            relays[index].start()

    for g in range(3):
        gy_send(g)
    for g in range(3):
        gy_pass(g)

    mirror_gain = send(gsend, grecv, m_s.at[4], m_r.at[4], mirror)
    gain_sum = None
    for g, slot in ((0, 1), (1, 0)):
        gc_wait(g)
        scaled_cot = dot(full[g, :, lat:two], wd_ref[slot], 1, 1)
        wide = stash_ref[slot].astype(F32)
        pull = full[g, :, two : two + 1].astype(F32)
        rows_out[g] = (
            cot_ref[slot].astype(F32) + scaled_cot * gain_ref[slot : slot + 1, :] - wide * pull
        ).astype(BF16)
        relay_start(g)
        gain_rows = jnp.sum(wide * scaled_cot, axis=0, keepdims=True)
        if slot == 1:
            gsend[...] = jnp.broadcast_to(gain_rows, gsend.shape)
            mirror_gain.start()
        else:
            gain_sum = gain_rows
    gc_wait(2)
    for slot in range(2):
        branch = dot(full[2, :, slot * lat : (slot + 1) * lat], wu_ref[slot], 1, 0).astype(BF16)
        rows_out[2 + slot] = (fwd_ref[slot].astype(F32) + branch.astype(F32)).astype(BF16)
        relay_start(2 + slot)

    mirror_rows.wait_recv()
    gx_send(3)
    down_acc[...] = dot(zg[0], full[1, :, lat:two], 0, 0)
    gy_send(3)
    up_acc[...] = dot(full[1, :, :lat], cot_ref[0], 0, 0)
    gy_pass(3)
    gc_wait(3)

    factor = tokens ** (-0.5)
    mirror_dy.wait_recv()
    up = up_acc[:, :main] + dot(full[3, :, :lat], md[...], 0, 0)
    gu_out[:, :main] = (up * factor).astype(BF16)
    mirror_z.wait_recv()
    down = down_acc[:main, :] + dot(mz[...], full[3, :, lat:two], 0, 0)
    gd_out[:main, :] = (down * factor).astype(BF16)
    mirror_t.wait_recv()
    up = up_acc[:, main:] + dot(full[3, :, :lat], mt[...], 0, 0)[:, :rest]
    gu_out[:, main:] = (up * factor).astype(BF16)
    down = down_acc[main:, :] + dot(mt[...], full[3, :, lat:two], 0, 0)[rest:, :]
    gd_out[main:, :] = (down * factor).astype(BF16)
    mirror_gain.wait_recv()
    gg_out[...] = ((gain_sum + grecv[0:1, :]) * factor).astype(BF16)

    def edge(here, first, second):
        @pl.when(here)
        def _():
            zg[0] = jnp.zeros((tokens, cols), BF16)
            one = pltpu.make_async_copy(zg.at[0], first, zero_sem.at[0])
            other = pltpu.make_async_copy(zg.at[0], second, zero_sem.at[1])
            one.start()
            other.start()
            one.wait()
            other.wait()

    edge(pos == 0, fwd_out.at[0], bwd_out.at[1])
    edge(pos == n_pipe - 1, fwd_out.at[1], bwd_out.at[0])

    for index in range(4):
        @pl.when(ups[index % 2])
        def _():
            relays[index].wait_send()

        @pl.when(ups[1 - index % 2])
        def _():
            relays[index].wait_recv()

    for copy in [
        mirror_dy,
        mirror_z,
        mirror_t,
        mirror_rows,
        mirror_gain,
        *core_copies,
        *ring_copies,
        *x_copies,
        *gx_copies.values(),
        *gy_copies.values(),
        *gc_copies.values(),
    ]:
        copy.wait_send()


def per_device(n_pipe, fwd_in, stash, cot_in, w_down, w_up, gain):
    tokens, cols = stash.shape[2:]
    lat = w_down.shape[3]
    wide = 2 * lat + 128
    main = cols // 128 * 128
    half, quarter, own = tokens // 2, tokens // 8, tokens // 16
    vmem = pl.BlockSpec(memory_space=pltpu.VMEM)
    anywhere = pl.BlockSpec(memory_space=pl.ANY)
    dma = pltpu.SemaphoreType.DMA
    outs = pl.pallas_call(
        functools.partial(kernel, n_pipe),
        out_shape=(
            jax.ShapeDtypeStruct((2, tokens, cols), BF16),
            jax.ShapeDtypeStruct((2, tokens, cols), BF16),
            jax.ShapeDtypeStruct((cols, lat), BF16),
            jax.ShapeDtypeStruct((lat, cols), BF16),
            jax.ShapeDtypeStruct((1, cols), BF16),
        ),
        in_specs=[vmem] * 6,
        out_specs=(anywhere, anywhere, vmem, vmem, vmem),
        scratch_shapes=[
            pltpu.VMEM((3, tokens, wide), BF16),
            pltpu.VMEM((3, half, wide), BF16),
            pltpu.VMEM((3, Y - 1, quarter, wide), BF16),
            pltpu.VMEM((3, quarter, wide), BF16),
            pltpu.VMEM((3, own, wide), BF16),
            pltpu.VMEM((4, tokens, wide), BF16),
            pltpu.VMEM((2, tokens, cols), BF16),
            pltpu.VMEM((tokens, 128), BF16),
            pltpu.VMEM((tokens, main), BF16),
            pltpu.VMEM((tokens, main), BF16),
            pltpu.VMEM((tokens, 128), BF16),
            pltpu.VMEM((8, cols), F32),
            pltpu.VMEM((8, cols), F32),
            pltpu.VMEM((4, tokens, cols), BF16),
            pltpu.VMEM((cols, lat), F32),
            pltpu.VMEM((lat, cols), F32),
            dma((3,)),
            dma((3,)),
            dma((3, Y - 1)),
            dma((3, Y - 1)),
            dma((3,)),
            dma((3,)),
            dma((4,)),
            dma((4,)),
            dma((4, Y - 1)),
            dma((4, Y - 1)),
            dma((4, Y)),
            dma((4, Y)),
            dma((5,)),
            dma((5,)),
            dma((4,)),
            dma((4,)),
            dma((2,)),
        ],
        compiler_params=pltpu.CompilerParams(
            collective_id=0, has_side_effects=True, vmem_limit_bytes=40 * 1024 * 1024
        ),
    )(fwd_in[0], stash[0], cot_in[0], w_down[0], w_up[0], gain[0])
    fwd_next, bwd_next, grad_down, grad_up, grad_gain = outs
    return (fwd_next[None], bwd_next[None], grad_down[None], grad_up[None], grad_gain)


def solution(mesh):
    placed = (
        P("pipe", None, None, "dp"),
        P("pipe", None, None, "dp"),
        P("pipe", None, None, "dp"),
        P("pipe", None, "dp", None),
        P("pipe", None, None, "dp"),
        P("pipe", None, "dp"),
    )
    return jax.shard_map(
        functools.partial(per_device, mesh.shape["pipe"]),
        mesh=mesh,
        in_specs=placed,
        out_specs=(
            P("pipe", None, None, "dp"),
            P("pipe", None, None, "dp"),
            P("pipe", "dp", None),
            P("pipe", None, "dp"),
            P("pipe", "dp"),
        ),
        check_vma=False,
    )
```

time: 583 us -> 101 us (0.17)
  the two profiles are of different devices: /device:TPU:3 before, /device:TPU:1 now
where the time goes in v1:
time: 101 us; the launch traced here: 100 us
  Pallas kernels  87 us (86%)
  local copies, waits for them, and re-layouts  12.7 us (13%)
    pallas_call x1, Pallas kernels, per_device(): pl.pallas_call(functools.partial(kernel, n_pipe), out_shape=(jax.ShapeDty...  87 us
    unnamed x31, local copies, waits for them, and re-layouts  12.7 us

profile of v1, /device:TPU:1, one launch (start us, length us, event | category | flops | bytes accessed | tf_op | source)
XLA Modules:
  0.0 100.4 jit_solution(10069861913511070000)
XLA Ops:
  0.6 0.0 copy-start.9
  0.6 1.3 %copy.11 = bf16[1,2,256,448]{3,2,1,0:T(8,128)(2,1)S(1)} copy(bf16[1,2,256,448]{2,3,1,0:T(8,128)(2,1)} %param.6) | data formatting | bytes 917504 | tf_op args[0]
  1.9 0.0 copy-done.9
  1.9 0.0 copy-start.10
  1.9 0.2 copy.12
  2.2 0.8 copy-done.10
  3.0 0.2 copy.13
  3.2 0.0 copy-start
  3.2 0.0 copy-start.8
  3.2 1.5 %copy.14 = bf16[1,2,512,448]{3,2,1,0:T(8,128)(2,1)S(1)} copy(bf16[1,2,512,448]{2,3,1,0:T(8,128)(2,1)} %param.10) | data formatting | bytes 1835008 | tf_op args[4]
  4.7 0.0 copy-done
  4.7 0.0 copy-done.8
  4.8 87.0 %shard_map.101 = (bf16[2,256,448]{2,1,0:T(8,128)(2,1)S(1)}, bf16[2,256,448]{2,1,0:T(8,128)(2,1)S(1)}, bf16[448,512]{1,0:T(8,128)(2,1)S(1)}, bf16[512,448]{1,0:T(8,128)(2,1)S(1)}, bf16[1,448]{1,0:T(2,128)(2,1)S(1)}) custom-call(bf16[2,256,448]{2,1,0:T(8,128)(2,1)S(1)} %bitcast.11, bf16[2,256,448]{2,1,0:T(8,128)(2,1)S(1)} %bitcast.12, ...), custom_call_target="tpu_custom_call" | custom-call | tf_op jit(solution)/shard_map/pallas_call | solution.py:358
  91.7 0.0 copy-start.1
  91.7 0.8 copy-done.1
  92.5 0.0 copy-start.3
  92.5 0.8 copy-done.3
  93.3 0.0 copy-start.5
  93.3 0.8 copy-done.5
  94.1 0.0 copy-start.6
  94.1 0.8 copy-done.6
  94.9 0.0 copy-start.4
  94.9 2.1 %copy.15 = bf16[1,2,256,448]{2,3,1,0:T(8,128)(2,1)} copy(bf16[1,2,256,448]{3,2,1,0:T(8,128)(2,1)} %bitcast.17) | data formatting | bytes 917504
  97.0 0.0 copy-start.2
  97.0 0.0 copy-done.4
  97.0 1.0 copy.16
  97.9 0.1 copy-done.2
  98.0 0.0 copy-start.7
  98.0 1.0 copy.17
  99.0 0.1 copy-done.7
  99.0 0.8 copy.20
  99.8 0.6 copy.21
Async XLA Ops:
  0.6 1.3 %copy-start.9 = (bf16[1,2,256,448]{2,3,1,0:T(8,128)(2,1)S(1)}, bf16[1,2,256,448]{2,3,1,0:T(8,128)(2,1)}, u32[]{:S(2)}) copy-start(bf16[1,2,256,448]{2,3,1,0:T(8,128)(2,1)} %param.7) | copy-start | bytes 1376260
  1.9 1.0 %copy-start.10 = (bf16[1,2,256,448]{2,3,1,0:T(8,128)(2,1)S(1)}, bf16[1,2,256,448]{2,3,1,0:T(8,128)(2,1)}, u32[]{:S(2)}) copy-start(bf16[1,2,256,448]{2,3,1,0:T(8,128)(2,1)} %param.8) | copy-start | bytes 1376260
  3.2 1.6 %copy-start = (bf16[1,2,448,512]{3,2,1,0:T(8,128)(2,1)S(1)}, bf16[1,2,448,512]{3,2,1,0:T(8,128)(2,1)}, u32[]{:S(2)}) copy-start(bf16[1,2,448,512]{3,2,1,0:T(8,128)(2,1)} %param.9) | copy-start | bytes 2752516
  3.2 1.6 %copy-start.8 = (f32[1,2,448]{2,1,0:T(2,128)S(1)}, f32[1,2,448]{2,1,0:T(2,128)}, u32[]{:S(2)}) copy-start(f32[1,2,448]{2,1,0:T(2,128)} %param.11) | copy-start | bytes 10756
  91.7 0.8 copy-start.1
  92.5 0.8 copy-start.3
  93.3 0.8 copy-start.5
  94.1 0.8 copy-start.6
  94.9 2.1 %copy-start.4 = (bf16[2,256,448]{2,1,0:T(8,128)(2,1)S(1)}, bf16[2,256,448]{2,1,0:T(8,128)(2,1)}, u32[]{:S(2)}) copy-start(bf16[2,256,448]{2,1,0:T(8,128)(2,1)} %copy-done.3) | copy-start | bytes 1376260
  97.0 1.0 %copy-start.2 = (bf16[512,448]{1,0:T(8,128)(2,1)S(1)}, bf16[512,448]{1,0:T(8,128)(2,1)}, u32[]{:S(2)}) copy-start(bf16[512,448]{1,0:T(8,128)(2,1)} %copy-done.1) | copy-start | bytes 1376260
  98.0 1.0 %copy-start.7 = (bf16[448,512]{1,0:T(8,128)(2,1)S(1)}, bf16[448,512]{1,0:T(8,128)(2,1)}, u32[]{:S(2)}) copy-start(bf16[448,512]{1,0:T(8,128)(2,1)} %copy-done.6) | copy-start | bytes 1376260

commit v2 on v1

v2 whole, which is shorter than its diff:
```python
import functools

import jax
import jax.numpy as jnp
from jax import lax
from jax.experimental import pallas as pl
from jax.experimental.pallas import tpu as pltpu
from jax.sharding import PartitionSpec as P

MESH = pl.DeviceIdType.MESH
EPS = 1e-06
BF16 = jnp.bfloat16
F32 = jnp.float32

Y, XH, CORE = 4, 2, 2


def dot(a, b, ca, cb):
    return lax.dot_general(a, b, (((ca,), (cb,)), ((), ())), preferred_element_type=F32)


def kernel(
    n_pipe,
    fwd_hbm,
    stash_hbm,
    cot_hbm,
    wd_hbm,
    wu_hbm,
    gain_ref,
    fwd_out,
    bwd_out,
    gd_out,
    gu_out,
    gg_out,
    fwd_ref,
    stash_ref,
    cot_ref,
    wd_ref,
    wu_ref,
    part,
    r1,
    ra,
    rb,
    fa,
    fb,
    h2,
    r3,
    full,
    zg,
    mz,
    md,
    gsend,
    grecv,
    rows_out,
    down_acc,
    up_acc,
    in_sem,
    core_s,
    core_r,
    ya_s,
    ya_r,
    yb_s,
    yb_r,
    x_s,
    x_r,
    gx_s,
    gx_r,
    gy_s,
    gy_r,
    gc_s,
    gc_r,
    m_s,
    m_r,
    n_s,
    n_r,
    zero_sem,
):
    pos = lax.axis_index("pipe")
    d = lax.axis_index("dp")
    cols, tokens = stash_ref.shape[1:]
    lat = wd_ref.shape[2]
    features = cols * Y * XH * CORE
    two = 2 * lat
    half, quarter, own = tokens // 2, tokens // 8, tokens // 16
    core = d % CORE
    xh = d // CORE % XH
    y = d // (CORE * XH)
    sibling = (pos, d + 1 - 2 * core)
    across = (pos, d + CORE * (1 - 2 * xh))
    y1, y2, y3 = y + 1 - 2 * (y % 2), (y + 2) % Y, Y - 1 - y
    side1 = (pos, y1 * (CORE * XH) + d % (CORE * XH))
    side3 = (pos, y3 * (CORE * XH) + d % (CORE * XH))
    mirror = (n_pipe - 1 - pos, d)
    above = ((pos + 1) % n_pipe, d)
    below = ((pos + n_pipe - 1) % n_pipe, d)

    def send(src, dst, s_sem, r_sem, device):
        return pltpu.make_async_remote_copy(
            src_ref=src,
            dst_ref=dst,
            send_sem=s_sem,
            recv_sem=r_sem,
            device_id=device,
            device_id_type=MESH,
        )

    loads = {}
    for index, (name, src, dst) in enumerate(
        (
            ("cot1", cot_hbm.at[1], cot_ref.at[1]),
            ("stash1", stash_hbm.at[1], stash_ref.at[1]),
            ("wd", wd_hbm, wd_ref),
            ("wu", wu_hbm, wu_ref),
            ("stash0", stash_hbm.at[0], stash_ref.at[0]),
            ("cot0", cot_hbm.at[0], cot_ref.at[0]),
            ("fwd", fwd_hbm, fwd_ref),
        )
    ):
        loads[name] = pltpu.make_async_copy(src, dst, in_sem.at[index])
        loads[name].start()

    barrier = pltpu.get_barrier_semaphore()
    partners = [sibling, across, side1, side3, mirror, above, below]
    for device in partners:
        pl.semaphore_signal(barrier, inc=1, device_id=device, device_id_type=MESH)

    def column(slot):
        wide = jnp.broadcast_to(gain_ref[slot : slot + 1, :], (128, cols)).T
        return jnp.concatenate([wide] * (tokens // 128), axis=1)

    gains = [column(0), column(1)]
    loads["stash1"].wait()
    zg[1] = (stash_ref[1].astype(F32) * gains[1]).astype(BF16)
    loads["cot1"].wait()

    mirror_dy = send(cot_ref.at[1], md, m_s.at[0], m_r.at[0], mirror)
    mirror_z = send(zg.at[1], mz, m_s.at[1], m_r.at[1], mirror)

    def squares(wide):
        ones = jnp.ones((cols, 128), BF16)
        return dot((wide * wide).astype(BF16), ones, 0, 0)

    core_copies = []
    sums_wide = (two + 128, two, two)

    def core_send(g):
        away = pl.multiple_of((1 - core) * half, half)
        copy = send(
            part.at[g, pl.ds(away, half), : sums_wide[g]],
            r1.at[g, :, : sums_wide[g]],
            core_s.at[g],
            core_r.at[g],
            sibling,
        )
        copy.start()
        core_copies.append(copy)

    def partial_sums(g):
        if g == 0:
            loads["wd"].wait()
            part[0, :, :lat] = dot(zg[1], wd_ref[1], 0, 0).astype(BF16)
            loads["wu"].wait()
            part[0, :, lat:two] = dot(cot_ref[1], wu_ref[1], 0, 0).astype(BF16)
            loads["stash0"].wait()
            loads["fwd"].wait()
            lane = lax.broadcasted_iota(jnp.int32, (tokens, 128), 1)
            norms = squares(stash_ref[1].astype(F32))
            for index, array in enumerate((stash_ref.at[0], fwd_ref.at[0], fwd_ref.at[1])):
                norms = jnp.where(lane < 32 * (index + 1), norms, squares(array[...].astype(F32)))
            part[0, :, two:] = norms.astype(BF16)
        elif g == 1:
            zg[0] = (stash_ref[0].astype(F32) * gains[0]).astype(BF16)
            part[1, :, :lat] = dot(zg[0], wd_ref[0], 0, 0).astype(BF16)
            loads["cot0"].wait()
            part[1, :, lat:two] = dot(cot_ref[0], wu_ref[0], 0, 0).astype(BF16)
        else:
            for slot in range(2):
                rows = (fwd_ref[slot].astype(F32) * gains[slot]).astype(BF16)
                part[2, :, slot * lat : (slot + 1) * lat] = dot(rows, wd_ref[slot], 0, 0).astype(BF16)

    for g in range(3):
        partial_sums(g)
    pl.semaphore_wait(barrier, len(partners))
    mirror_dy.start()

    def rows_of(index):
        return pl.ds(pl.multiple_of(index * quarter, quarter), quarter)

    ya_copies, yb_copies = {}, {}

    def a_send(g, index, src, device):
        ya_copies[g, index] = send(src, ra.at[g, index], ya_s.at[g, index], ya_r.at[g, index], device)
        ya_copies[g, index].start()

    def b_send(g, index, src, device):
        spot = rb.at[g, index, :, : sums_wide[g] - lat]
        yb_copies[g, index] = send(src, spot, yb_s.at[g, index], yb_r.at[g, index], device)
        yb_copies[g, index].start()

    def core_sum(g):
        wide = sums_wide[g]
        core_copies[g].wait_recv()
        mine = part[g, pl.ds(pl.multiple_of(core * half, half), half), :wide].astype(F32)
        r1[g, :, :wide] = (mine + r1[g, :, :wide].astype(F32)).astype(BF16)
        a_send(g, 0, r1.at[g, rows_of(y2), :lat], side1)
        b_send(g, 0, r1.at[g, rows_of(y2), lat:wide], side3)
        a_send(g, 1, r1.at[g, rows_of(y1), :lat], side1)
        b_send(g, 1, r1.at[g, rows_of(y3), lat:wide], side3)

    def y_first(g):
        wide = sums_wide[g]
        ya_copies[g, 0].wait_recv()
        fa[g] = (r1[g, rows_of(y3), :lat].astype(F32) + ra[g, 0].astype(F32)).astype(BF16)
        a_send(g, 2, fa.at[g], side3)
        yb_copies[g, 0].wait_recv()
        fb[g, :, : wide - lat] = (
            r1[g, rows_of(y1), lat:wide].astype(F32) + rb[g, 0, :, : wide - lat].astype(F32)
        ).astype(BF16)
        b_send(g, 2, fb.at[g, :, : wide - lat], side1)

    x_copies = []

    def y_second(g):
        wide = sums_wide[g]
        mine = r1[g, rows_of(y), :wide].astype(F32)
        for index in (1, 2):
            ya_copies[g, index].wait_recv()
            yb_copies[g, index].wait_recv()
        h2[g, :, :lat] = (mine[:, :lat] + ra[g, 1].astype(F32) + ra[g, 2].astype(F32)).astype(BF16)
        h2[g, :, lat:wide] = (
            mine[:, lat:] + rb[g, 1, :, : wide - lat].astype(F32) + rb[g, 2, :, : wide - lat].astype(F32)
        ).astype(BF16)
        copy = send(
            h2.at[g, pl.ds(pl.multiple_of((1 - xh) * own, own), own), :wide],
            r3.at[g, :, :wide],
            x_s.at[g],
            x_r.at[g],
            across,
        )
        copy.start()
        x_copies.append(copy)

    base = pl.multiple_of(core * half + y * quarter + xh * own, own)

    def mean_sq(values):
        return jnp.sum(values * values, axis=1, keepdims=True) / lat

    mirror_rows = send(
        full.at[0, pl.ds(base, own), :two],
        full.at[3, pl.ds(base, own), :two],
        m_s.at[2],
        m_r.at[2],
        mirror,
    )
    gx_copies = {}
    widths = (two + 128, two + 128, two, two)

    def gx_send(g):
        spot = full.at[g, pl.ds(base, own), : widths[g]]
        gx_copies[g] = send(spot, spot, gx_s.at[g], gx_r.at[g], across)
        gx_copies[g].start()

    squared = []

    def own_rows(g):
        wide = sums_wide[g]
        x_copies[g].wait_recv()
        total = h2[g, pl.ds(pl.multiple_of(xh * own, own), own), :wide].astype(F32)
        total = total + r3[g, :, :wide].astype(F32)
        first, second = total[:, :lat], total[:, lat:two]
        if g == 0:
            for k in range(4):
                squared.append(total[:, two + 32 * k : two + 32 * k + 1] / features + EPS)
        square = squared[g]
        scale = lax.rsqrt(mean_sq(first) + EPS * square)
        unit = first * scale
        full[g, pl.ds(base, own), :lat] = unit.astype(BF16)
        if g < 2:
            mean = jnp.sum(second * unit, axis=1, keepdims=True) / lat
            cot = (scale * (second - unit * mean)).astype(BF16)
            full[g, pl.ds(base, own), lat:two] = cot
            pull = jnp.sum(cot.astype(F32) * first, axis=1, keepdims=True) / (features * square)
            full[g, pl.ds(base, own), two:] = jnp.broadcast_to(pull, (own, 128)).astype(BF16)
        else:
            scale = lax.rsqrt(mean_sq(second) + EPS * squared[3])
            full[g, pl.ds(base, own), lat:two] = (second * scale).astype(BF16)
        if g == 0:
            mirror_rows.start()
        gx_send(g)

    gy_copies, gc_copies = {}, {}

    def block_of(index):
        return pl.ds(pl.multiple_of(core * half + index * quarter, quarter), quarter)

    def gc_send(g, index, block):
        spot = full.at[g, block_of(block), : widths[g]]
        gc_copies[g, index] = send(spot, spot, gc_s.at[g, index], gc_r.at[g, index], sibling)
        gc_copies[g, index].start()

    def gy_start(g, index, spot, device):
        gy_copies[g, index] = send(spot, spot, gy_s.at[g, index], gy_r.at[g, index], device)
        gy_copies[g, index].start()

    def gy_send(g):
        gx_copies[g].wait_recv()
        spot = full.at[g, block_of(y), : widths[g]]
        gy_start(g, 0, spot, side1)
        gy_start(g, 1, spot, side3)
        gc_send(g, 0, y)

    def gy_pass(g):
        gy_copies[g, 1].wait_recv()
        gy_start(g, 2, full.at[g, block_of(y3), :lat], side1)
        gy_copies[g, 0].wait_recv()
        gy_start(g, 3, full.at[g, block_of(y1), lat : widths[g]], side3)
        gc_send(g, 1, y3)
        gc_send(g, 2, y1)

    def gy_last(g):
        gy_copies[g, 2].wait_recv()
        gy_copies[g, 3].wait_recv()
        gc_send(g, 3, y2)

    def gc_wait(g):
        for k in range(Y):
            gc_copies[g, k].wait_recv()

    ups = (pos < n_pipe - 1, pos > 0)

    def relay(index, slot, out, up):
        return send(rows_out.at[index], out.at[slot], n_s.at[index], n_r.at[index], above if up else below)

    relays = [
        relay(0, 1, bwd_out, True),
        relay(1, 0, bwd_out, False),
        relay(2, 0, fwd_out, True),
        relay(3, 1, fwd_out, False),
    ]

    def relay_start(index):
        @pl.when(ups[index % 2])
        def _():
            relays[index].start()

    mirror_gain = send(gsend, grecv, m_s.at[3], m_r.at[3], mirror)
    pick = jnp.where(lax.broadcasted_iota(jnp.int32, (8, 128), 1) == 0, 1.0, 0.0).astype(BF16)
    gain_parts = {}

    def results(g):
        gc_wait(g)
        if g == 2:
            for slot in range(2):
                branch = dot(wu_ref[slot], full[2, :, slot * lat : (slot + 1) * lat], 1, 1).astype(BF16)
                rows_out[2 + slot] = (fwd_ref[slot].astype(F32) + branch.astype(F32)).astype(BF16)
                relay_start(2 + slot)
            return
        slot = 1 - g
        scaled_cot = dot(wd_ref[slot], full[g, :, lat:two], 1, 1)
        wide = stash_ref[slot].astype(F32)
        pull = dot(pick, full[g, :, two:], 1, 1)[0:1, :]
        rows_out[g] = (
            cot_ref[slot].astype(F32) + scaled_cot * gains[slot] - wide * pull
        ).astype(BF16)
        relay_start(g)
        products = (wide * scaled_cot).astype(BF16)
        gain_parts[slot] = dot(jnp.ones((8, tokens), BF16), products, 1, 1)

    stages = (
        core_send,
        core_sum,
        y_first,
        y_second,
        own_rows,
        gy_send,
        gy_pass,
        gy_last,
        results,
    )
    for g in range(3):
        core_send(g)
    for step in range(1, len(stages) + 3):
        for g in range(4):
            stage = step - g - g // 3
            if 0 < stage < len(stages):
                if g < 3:
                    stages[stage](g)
                elif stage == 4:
                    mirror_rows.wait_recv()
                    mirror_z.start()
                    gx_send(3)
                elif 4 < stage < len(stages) - 1:
                    stages[stage](3)

    gsend[...] = gain_parts[1]
    mirror_gain.start()
    down_acc[...] = dot(zg[0], full[1, :, lat:two], 1, 0)
    up_acc[...] = dot(cot_ref[0], full[1, :, :lat], 1, 0)
    gc_wait(3)

    factor = tokens ** (-0.5)
    mirror_dy.wait_recv()
    up = up_acc[...] + dot(md[...], full[3, :, :lat], 1, 0)
    gu_out[...] = (up * factor).astype(BF16)
    mirror_z.wait_recv()
    down = down_acc[...] + dot(mz[...], full[3, :, lat:two], 1, 0)
    gd_out[...] = (down * factor).astype(BF16)
    mirror_gain.wait_recv()
    gg_out[...] = ((gain_parts[0] + grecv[...])[0:1, :] * factor).astype(BF16)

    def edge(here, first, second):
        @pl.when(here)
        def _():
            zg[0] = jnp.zeros((cols, tokens), BF16)
            one = pltpu.make_async_copy(zg.at[0], first, zero_sem.at[0])
            other = pltpu.make_async_copy(zg.at[0], second, zero_sem.at[1])
            one.start()
            other.start()
            one.wait()
            other.wait()

    edge(pos == 0, fwd_out.at[0], bwd_out.at[1])
    edge(pos == n_pipe - 1, fwd_out.at[1], bwd_out.at[0])

    for index in range(4):

        @pl.when(ups[index % 2])
        def _():
            relays[index].wait_send()

        @pl.when(ups[1 - index % 2])
        def _():
            relays[index].wait_recv()

    for copy in [
        mirror_dy,
        mirror_z,
        mirror_rows,
        mirror_gain,
        *core_copies,
        *ya_copies.values(),
        *yb_copies.values(),
        *x_copies,
        *gx_copies.values(),
        *gy_copies.values(),
        *gc_copies.values(),
    ]:
        copy.wait_send()


def place(*refs):
    count = (len(refs) - 2) // 3
    sources, targets, held = refs[:count], refs[count : 2 * count], refs[2 * count : 3 * count]
    arrive, leave = refs[3 * count :]
    copies = []
    for index in range(count):
        first = pltpu.make_async_copy(sources[index], held[index], arrive.at[index])
        second = pltpu.make_async_copy(held[index], targets[index], leave.at[index])
        first.start()
        copies.append((first, second))
    for first, second in copies:
        first.wait()
        second.start()
    for first, second in copies:
        second.wait()


def per_device(n_pipe, fwd_in, stash, cot_in, w_down, w_up, gain):
    tokens, cols = stash.shape[2:]
    lat = w_down.shape[3]
    wide = 2 * lat + 128
    half, quarter, own = tokens // 2, tokens // 8, tokens // 16
    vmem = pl.BlockSpec(memory_space=pltpu.VMEM)
    anywhere = pl.BlockSpec(memory_space=pl.ANY)
    dma = pltpu.SemaphoreType.DMA
    turned = lambda array: jnp.swapaxes(array[0], 1, 2)
    outs = pl.pallas_call(
        functools.partial(kernel, n_pipe),
        out_shape=(
            jax.ShapeDtypeStruct((2, cols, tokens), BF16),
            jax.ShapeDtypeStruct((2, cols, tokens), BF16),
            jax.ShapeDtypeStruct((cols, lat), BF16),
            jax.ShapeDtypeStruct((cols, lat), BF16),
            jax.ShapeDtypeStruct((1, cols), BF16),
        ),
        in_specs=[anywhere] * 5 + [vmem],
        out_specs=(anywhere, anywhere, vmem, vmem, vmem),
        scratch_shapes=[
            pltpu.VMEM((2, cols, tokens), BF16),
            pltpu.VMEM((2, cols, tokens), BF16),
            pltpu.VMEM((2, cols, tokens), BF16),
            pltpu.VMEM((2, cols, lat), BF16),
            pltpu.VMEM((2, cols, lat), BF16),
            pltpu.VMEM((3, tokens, wide), BF16),
            pltpu.VMEM((3, half, wide), BF16),
            pltpu.VMEM((3, 3, quarter, lat), BF16),
            pltpu.VMEM((3, 3, quarter, lat + 128), BF16),
            pltpu.VMEM((3, quarter, lat), BF16),
            pltpu.VMEM((3, quarter, lat + 128), BF16),
            pltpu.VMEM((3, quarter, wide), BF16),
            pltpu.VMEM((3, own, wide), BF16),
            pltpu.VMEM((4, tokens, wide), BF16),
            pltpu.VMEM((2, cols, tokens), BF16),
            pltpu.VMEM((cols, tokens), BF16),
            pltpu.VMEM((cols, tokens), BF16),
            pltpu.VMEM((8, cols), F32),
            pltpu.VMEM((8, cols), F32),
            pltpu.VMEM((4, cols, tokens), BF16),
            pltpu.VMEM((cols, lat), F32),
            pltpu.VMEM((cols, lat), F32),
            dma((7,)),
            dma((3,)),
            dma((3,)),
            dma((3, 3)),
            dma((3, 3)),
            dma((3, 3)),
            dma((3, 3)),
            dma((3,)),
            dma((3,)),
            dma((4,)),
            dma((4,)),
            dma((4, Y)),
            dma((4, Y)),
            dma((4, Y)),
            dma((4, Y)),
            dma((4,)),
            dma((4,)),
            dma((4,)),
            dma((4,)),
            dma((2,)),
        ],
        compiler_params=pltpu.CompilerParams(
            collective_id=0, has_side_effects=True, vmem_limit_bytes=56 * 1024 * 1024
        ),
    )(turned(fwd_in), turned(stash), turned(cot_in), w_down[0], turned(w_up), gain[0])
    fwd_next, bwd_next, grad_down, grad_up, grad_gain = pl.pallas_call(
        place,
        out_shape=tuple(jax.ShapeDtypeStruct(array.shape, array.dtype) for array in outs),
        in_specs=[anywhere] * 5,
        out_specs=(anywhere,) * 5,
        scratch_shapes=[pltpu.VMEM(array.shape, array.dtype) for array in outs] + [dma((5,)), dma((5,))],
        compiler_params=pltpu.CompilerParams(vmem_limit_bytes=56 * 1024 * 1024),
    )(*outs)
    return (
        jnp.swapaxes(fwd_next, 1, 2)[None],
        jnp.swapaxes(bwd_next, 1, 2)[None],
        grad_down[None],
        grad_up.T[None],
        grad_gain,
    )


def solution(mesh):
    placed = (
        P("pipe", None, None, "dp"),
        P("pipe", None, None, "dp"),
        P("pipe", None, None, "dp"),
        P("pipe", None, "dp", None),
        P("pipe", None, None, "dp"),
        P("pipe", None, "dp"),
    )
    return jax.shard_map(
        functools.partial(per_device, mesh.shape["pipe"]),
        mesh=mesh,
        in_specs=placed,
        out_specs=(
            P("pipe", None, None, "dp"),
            P("pipe", None, None, "dp"),
            P("pipe", "dp", None),
            P("pipe", None, "dp"),
            P("pipe", "dp"),
        ),
        check_vma=False,
    )
```

time: 101 us -> 81.9 us (0.81)
  the two profiles are of different devices: /device:TPU:1 before, /device:TPU:73 now
where the time goes in v2:
time: 81.9 us; the launch traced here: 81.7 us
  Pallas kernels  81.1 us (99%)
    pallas_call x1, Pallas kernels, per_device(): pl.pallas_call(functools.partial(kernel, n_pipe), out_shape=(jax.ShapeDty...  78.7 us
    pallas_call x1, Pallas kernels, per_device(): pl.pallas_call(place, out_shape=tuple((jax.ShapeDtypeStruct(array.shape,...  2.33 us

profile of v2, /device:TPU:73, one launch (start us, length us, event | category | flops | bytes accessed | tf_op | source)
XLA Modules:
  0.0 81.7 jit_solution(2628830808753185898)
XLA Ops:
  0.6 78.7 %shard_map.101 = (bf16[2,448,256]{2,1,0:T(8,128)(2,1)}, bf16[2,448,256]{2,1,0:T(8,128)(2,1)}, bf16[448,512]{1,0:T(8,128)(2,1)}, bf16[448,512]{1,0:T(8,128)(2,1)}, bf16[1,448]{1,0:T(2,128)(2,1)}) custom-call(bf16[2,448,256]{2,1,0:T(8,128)(2,1)} %bitcast.26, bf16[2,448,256]{2,1,0:T(8,128)(2,1)} %bitcast.27, bf16[2,448,256]{2,1,0:T(8,128)(2,1)} %bitcast.28, ...), custom_call_target="tpu_custom_call" | custom-call | tf_op jit(solution)/shard_map/pallas_call | solution.py:477
  79.4 2.3 %shard_map.102 = (bf16[2,448,256]{2,1,0:T(8,128)(2,1)}, bf16[2,448,256]{2,1,0:T(8,128)(2,1)}, bf16[448,512]{1,0:T(8,128)(2,1)}, bf16[448,512]{1,0:T(8,128)(2,1)}, bf16[1,448]{1,0:T(2,128)(2,1)}) custom-call(bf16[2,448,256]{2,1,0:T(8,128)(2,1)} %get-tuple-element.15.refs_0_, bf16[2,448,256]{2,1,0:T(8,128)(2,1)} %get-tuple-element.16.refs_1_, ...), custom_call_target="tpu_custom_call" | custom-call | tf_op jit(solution)/shard_map/pallas_call | solution.py:536

commit v3 on v2

--- a/solution.py
+++ b/solution.py
@@ -39,28 +39,25 @@
     wu_ref,
     part,
     r1,
-    ra,
-    rb,
-    fa,
-    fb,
+    r2,
     h2,
     r3,
     full,
     zg,
     mz,
+    zx,
     md,
     gsend,
     grecv,
     rows_out,
     down_acc,
-    up_acc,
+    gd_held,
+    gu_held,
     in_sem,
     core_s,
     core_r,
-    ya_s,
-    ya_r,
-    yb_s,
-    yb_r,
+    y_s,
+    y_r,
     x_s,
     x_r,
     gx_s,
@@ -74,6 +71,7 @@
     n_s,
     n_r,
     zero_sem,
+    w_sem,
 ):
     pos = lax.axis_index("pipe")
     d = lax.axis_index("dp")
@@ -87,10 +85,10 @@
     y = d // (CORE * XH)
     sibling = (pos, d + 1 - 2 * core)
     across = (pos, d + CORE * (1 - 2 * xh))
-    y1, y2, y3 = y + 1 - 2 * (y % 2), (y + 2) % Y, Y - 1 - y
-    side1 = (pos, y1 * (CORE * XH) + d % (CORE * XH))
-    side3 = (pos, y3 * (CORE * XH) + d % (CORE * XH))
+    ring = [(pos, (y + k) % Y * (CORE * XH) + d % (CORE * XH)) for k in range(1, Y)]
     mirror = (n_pipe - 1 - pos, d)
+    beside = (pos + 1 - 2 * (pos % 2), d)
+    opposite = (n_pipe - 2 - pos + 2 * (pos % 2), d)
     above = ((pos + 1) % n_pipe, d)
     below = ((pos + n_pipe - 1) % n_pipe, d)
 
@@ -120,7 +118,7 @@
         loads[name].start()
 
     barrier = pltpu.get_barrier_semaphore()
-    partners = [sibling, across, side1, side3, mirror, above, below]
+    partners = [sibling, across, *ring, mirror, beside, opposite, above, below]
     for device in partners:
         pl.semaphore_signal(barrier, inc=1, device_id=device, device_id_type=MESH)
 
@@ -134,7 +132,8 @@
     loads["cot1"].wait()
 
     mirror_dy = send(cot_ref.at[1], md, m_s.at[0], m_r.at[0], mirror)
-    mirror_z = send(zg.at[1], mz, m_s.at[1], m_r.at[1], mirror)
+    mirror_z_first = send(zg.at[1], zx, m_s.at[4], m_r.at[4], beside)
+    mirror_z = send(zx, mz, m_s.at[1], m_r.at[1], opposite)
 
     def squares(wide):
         ones = jnp.ones((cols, 128), BF16)
@@ -165,71 +164,57 @@
             loads["fwd"].wait()
             lane = lax.broadcasted_iota(jnp.int32, (tokens, 128), 1)
             norms = squares(stash_ref[1].astype(F32))
-            for index, array in enumerate((stash_ref.at[0], fwd_ref.at[0], fwd_ref.at[1])):
+            for index, array in enumerate((fwd_ref.at[0], fwd_ref.at[1], stash_ref.at[0])):
                 norms = jnp.where(lane < 32 * (index + 1), norms, squares(array[...].astype(F32)))
             part[0, :, two:] = norms.astype(BF16)
-        elif g == 1:
+        elif g == 2:
             zg[0] = (stash_ref[0].astype(F32) * gains[0]).astype(BF16)
-            part[1, :, :lat] = dot(zg[0], wd_ref[0], 0, 0).astype(BF16)
+            part[2, :, :lat] = dot(zg[0], wd_ref[0], 0, 0).astype(BF16)
             loads["cot0"].wait()
-            part[1, :, lat:two] = dot(cot_ref[0], wu_ref[0], 0, 0).astype(BF16)
+            part[2, :, lat:two] = dot(cot_ref[0], wu_ref[0], 0, 0).astype(BF16)
         else:
             for slot in range(2):
                 rows = (fwd_ref[slot].astype(F32) * gains[slot]).astype(BF16)
-                part[2, :, slot * lat : (slot + 1) * lat] = dot(rows, wd_ref[slot], 0, 0).astype(BF16)
-
-    for g in range(3):
-        partial_sums(g)
+                part[1, :, slot * lat : (slot + 1) * lat] = dot(rows, wd_ref[slot], 0, 0).astype(BF16)
+
+    partial_sums(0)
     pl.semaphore_wait(barrier, len(partners))
     mirror_dy.start()
+    mirror_z_first.start()
+    core_send(0)
+    for g in (1, 2):
+        partial_sums(g)
+        core_send(g)
 
     def rows_of(index):
         return pl.ds(pl.multiple_of(index * quarter, quarter), quarter)
 
-    ya_copies, yb_copies = {}, {}
-
-    def a_send(g, index, src, device):
-        ya_copies[g, index] = send(src, ra.at[g, index], ya_s.at[g, index], ya_r.at[g, index], device)
-        ya_copies[g, index].start()
-
-    def b_send(g, index, src, device):
-        spot = rb.at[g, index, :, : sums_wide[g] - lat]
-        yb_copies[g, index] = send(src, spot, yb_s.at[g, index], yb_r.at[g, index], device)
-        yb_copies[g, index].start()
+    y_copies = {}
 
     def core_sum(g):
         wide = sums_wide[g]
         core_copies[g].wait_recv()
         mine = part[g, pl.ds(pl.multiple_of(core * half, half), half), :wide].astype(F32)
         r1[g, :, :wide] = (mine + r1[g, :, :wide].astype(F32)).astype(BF16)
-        a_send(g, 0, r1.at[g, rows_of(y2), :lat], side1)
-        b_send(g, 0, r1.at[g, rows_of(y2), lat:wide], side3)
-        a_send(g, 1, r1.at[g, rows_of(y1), :lat], side1)
-        b_send(g, 1, r1.at[g, rows_of(y3), lat:wide], side3)
-
-    def y_first(g):
+        for k in range(Y - 1):
+            y_copies[g, k] = send(
+                r1.at[g, rows_of((y + k + 1) % Y), :wide],
+                r2.at[g, k, :, :wide],
+                y_s.at[g, k],
+                y_r.at[g, k],
+                ring[k],
+            )
+            y_copies[g, k].start()
+
+    x_copies = []
+
+    def y_sum(g):
         wide = sums_wide[g]
-        ya_copies[g, 0].wait_recv()
-        fa[g] = (r1[g, rows_of(y3), :lat].astype(F32) + ra[g, 0].astype(F32)).astype(BF16)
-        a_send(g, 2, fa.at[g], side3)
-        yb_copies[g, 0].wait_recv()
-        fb[g, :, : wide - lat] = (
-            r1[g, rows_of(y1), lat:wide].astype(F32) + rb[g, 0, :, : wide - lat].astype(F32)
-        ).astype(BF16)
-        b_send(g, 2, fb.at[g, :, : wide - lat], side1)
-
-    x_copies = []
-
-    def y_second(g):
-        wide = sums_wide[g]
-        mine = r1[g, rows_of(y), :wide].astype(F32)
-        for index in (1, 2):
-            ya_copies[g, index].wait_recv()
-            yb_copies[g, index].wait_recv()
-        h2[g, :, :lat] = (mine[:, :lat] + ra[g, 1].astype(F32) + ra[g, 2].astype(F32)).astype(BF16)
-        h2[g, :, lat:wide] = (
-            mine[:, lat:] + rb[g, 1, :, : wide - lat].astype(F32) + rb[g, 2, :, : wide - lat].astype(F32)
-        ).astype(BF16)
+        total = r1[g, rows_of(y), :wide].astype(F32)
+        for k in range(Y - 1):
+            y_copies[g, k].wait_recv()
+            total = total + r2[g, k, :, :wide].astype(F32)
+        h2[g, :, :wide] = total.astype(BF16)
         copy = send(
             h2.at[g, pl.ds(pl.multiple_of((1 - xh) * own, own), own), :wide],
             r3.at[g, :, :wide],
@@ -253,10 +238,10 @@
         mirror,
     )
     gx_copies = {}
-    widths = (two + 128, two + 128, two, two)
+    spans = ((lat, two + 128), (0, two), (lat, two + 128), (0, two + lat))
 
     def gx_send(g):
-        spot = full.at[g, pl.ds(base, own), : widths[g]]
+        spot = full.at[g, pl.ds(base, own), spans[g][0] : spans[g][1]]
         gx_copies[g] = send(spot, spot, gx_s.at[g], gx_r.at[g], across)
         gx_copies[g].start()
 
@@ -271,19 +256,22 @@
         if g == 0:
             for k in range(4):
                 squared.append(total[:, two + 32 * k : two + 32 * k + 1] / features + EPS)
-        square = squared[g]
+        square = squared[(0, 1, 3)[g]]
         scale = lax.rsqrt(mean_sq(first) + EPS * square)
         unit = first * scale
-        full[g, pl.ds(base, own), :lat] = unit.astype(BF16)
-        if g < 2:
+        if g == 2:
+            full[3, pl.ds(base, own), two : two + lat] = unit.astype(BF16)
+        else:
+            full[g, pl.ds(base, own), :lat] = unit.astype(BF16)
+        if g == 1:
+            scale = lax.rsqrt(mean_sq(second) + EPS * squared[2])
+            full[g, pl.ds(base, own), lat:two] = (second * scale).astype(BF16)
+        else:
             mean = jnp.sum(second * unit, axis=1, keepdims=True) / lat
             cot = (scale * (second - unit * mean)).astype(BF16)
             full[g, pl.ds(base, own), lat:two] = cot
             pull = jnp.sum(cot.astype(F32) * first, axis=1, keepdims=True) / (features * square)
-            full[g, pl.ds(base, own), two:] = jnp.broadcast_to(pull, (own, 128)).astype(BF16)
-        else:
-            scale = lax.rsqrt(mean_sq(second) + EPS * squared[3])
-            full[g, pl.ds(base, own), lat:two] = (second * scale).astype(BF16)
+            full[g, pl.ds(base, own), two : two + 128] = jnp.broadcast_to(pull, (own, 128)).astype(BF16)
         if g == 0:
             mirror_rows.start()
         gx_send(g)
@@ -294,33 +282,22 @@
         return pl.ds(pl.multiple_of(core * half + index * quarter, quarter), quarter)
 
     def gc_send(g, index, block):
-        spot = full.at[g, block_of(block), : widths[g]]
+        spot = full.at[g, block_of(block), spans[g][0] : spans[g][1]]
         gc_copies[g, index] = send(spot, spot, gc_s.at[g, index], gc_r.at[g, index], sibling)
         gc_copies[g, index].start()
 
-    def gy_start(g, index, spot, device):
-        gy_copies[g, index] = send(spot, spot, gy_s.at[g, index], gy_r.at[g, index], device)
-        gy_copies[g, index].start()
-
     def gy_send(g):
         gx_copies[g].wait_recv()
-        spot = full.at[g, block_of(y), : widths[g]]
-        gy_start(g, 0, spot, side1)
-        gy_start(g, 1, spot, side3)
+        spot = full.at[g, block_of(y), spans[g][0] : spans[g][1]]
+        for k in range(Y - 1):
+            gy_copies[g, k] = send(spot, spot, gy_s.at[g, k], gy_r.at[g, k], ring[k])
+            gy_copies[g, k].start()
         gc_send(g, 0, y)
 
     def gy_pass(g):
-        gy_copies[g, 1].wait_recv()
-        gy_start(g, 2, full.at[g, block_of(y3), :lat], side1)
-        gy_copies[g, 0].wait_recv()
-        gy_start(g, 3, full.at[g, block_of(y1), lat : widths[g]], side3)
-        gc_send(g, 1, y3)
-        gc_send(g, 2, y1)
-
-    def gy_last(g):
-        gy_copies[g, 2].wait_recv()
-        gy_copies[g, 3].wait_recv()
-        gc_send(g, 3, y2)
+        for k in range(1, Y):
+            gy_copies[g, k - 1].wait_recv()
+            gc_send(g, k, (y + Y - k) % Y)
 
     def gc_wait(g):
         for k in range(Y):
@@ -349,62 +326,61 @@
 
     def results(g):
         gc_wait(g)
-        if g == 2:
+        if g == 1:
             for slot in range(2):
-                branch = dot(wu_ref[slot], full[2, :, slot * lat : (slot + 1) * lat], 1, 1).astype(BF16)
+                branch = dot(wu_ref[slot], full[1, :, slot * lat : (slot + 1) * lat], 1, 1).astype(BF16)
                 rows_out[2 + slot] = (fwd_ref[slot].astype(F32) + branch.astype(F32)).astype(BF16)
                 relay_start(2 + slot)
             return
-        slot = 1 - g
+        slot = 1 - g // 2
         scaled_cot = dot(wd_ref[slot], full[g, :, lat:two], 1, 1)
         wide = stash_ref[slot].astype(F32)
-        pull = dot(pick, full[g, :, two:], 1, 1)[0:1, :]
-        rows_out[g] = (
+        pull = dot(pick, full[g, :, two : two + 128], 1, 1)[0:1, :]
+        rows_out[1 - slot] = (
             cot_ref[slot].astype(F32) + scaled_cot * gains[slot] - wide * pull
         ).astype(BF16)
-        relay_start(g)
+        relay_start(1 - slot)
         products = (wide * scaled_cot).astype(BF16)
         gain_parts[slot] = dot(jnp.ones((8, tokens), BF16), products, 1, 1)
 
-    stages = (
-        core_send,
-        core_sum,
-        y_first,
-        y_second,
-        own_rows,
-        gy_send,
-        gy_pass,
-        gy_last,
-        results,
-    )
-    for g in range(3):
-        core_send(g)
-    for step in range(1, len(stages) + 3):
-        for g in range(4):
-            stage = step - g - g // 3
-            if 0 < stage < len(stages):
-                if g < 3:
-                    stages[stage](g)
-                elif stage == 4:
-                    mirror_rows.wait_recv()
-                    mirror_z.start()
-                    gx_send(3)
-                elif 4 < stage < len(stages) - 1:
-                    stages[stage](3)
-
+    core_sum(0)
+    core_sum(1)
+    y_sum(0)
+    core_sum(2)
+    y_sum(1)
+    own_rows(0)
+    y_sum(2)
+    for stage in (own_rows, gy_send, gy_pass):
+        for g in range(3):
+            if g or stage is not own_rows:
+                stage(g)
+    mirror_rows.wait_recv()
+    mirror_z_first.wait_recv()
+    mirror_z.start()
+    gx_send(3)
+    results(0)
+    gy_send(3)
+    results(1)
+    gy_pass(3)
+    results(2)
     gsend[...] = gain_parts[1]
     mirror_gain.start()
-    down_acc[...] = dot(zg[0], full[1, :, lat:two], 1, 0)
-    up_acc[...] = dot(cot_ref[0], full[1, :, :lat], 1, 0)
+    down_acc[...] = dot(zg[0], full[2, :, lat:two], 1, 0)
     gc_wait(3)
 
     factor = tokens ** (-0.5)
     mirror_dy.wait_recv()
-    up = up_acc[...] + dot(md[...], full[3, :, :lat], 1, 0)
-    gu_out[...] = (up * factor).astype(BF16)
+    up = dot(cot_ref[0], full[3, :, two : two + lat], 1, 0) + dot(md[...], full[3, :, :lat], 1, 0)
+    gu_held[...] = (up * factor).astype(BF16)
+    leaving = [pltpu.make_async_copy(gu_held, gu_out, w_sem.at[0])]
+    leaving[0].start()
     mirror_z.wait_recv()
-    down = down_acc[...] + dot(mz[...], full[3, :, lat:two], 1, 0)
-    gd_out[...] = (down * factor).astype(BF16)
+    for index in range(2):
+        rows = pl.ds(index * (cols // 2), cols // 2)
+        down = down_acc[rows, :] + dot(mz[rows, :], full[3, :, lat:two], 1, 0)
+        gd_held[rows, :] = (down * factor).astype(BF16)
+        leaving.append(pltpu.make_async_copy(gd_held.at[rows], gd_out.at[rows], w_sem.at[index + 1]))
+        leaving[-1].start()
     mirror_gain.wait_recv()
     gg_out[...] = ((gain_parts[0] + grecv[...])[0:1, :] * factor).astype(BF16)
 
@@ -422,6 +398,8 @@
     edge(pos == 0, fwd_out.at[0], bwd_out.at[1])
     edge(pos == n_pipe - 1, fwd_out.at[1], bwd_out.at[0])
 
+    for copy in leaving:
+        copy.wait()
     for index in range(4):
 
         @pl.when(ups[index % 2])
@@ -435,11 +413,11 @@
     for copy in [
         mirror_dy,
         mirror_z,
+        mirror_z_first,
         mirror_rows,
         mirror_gain,
         *core_copies,
-        *ya_copies.values(),
-        *yb_copies.values(),
+        *y_copies.values(),
         *x_copies,
         *gx_copies.values(),
         *gy_copies.values(),
@@ -484,7 +462,7 @@
             jax.ShapeDtypeStruct((1, cols), BF16),
         ),
         in_specs=[anywhere] * 5 + [vmem],
-        out_specs=(anywhere, anywhere, vmem, vmem, vmem),
+        out_specs=(anywhere,) * 4 + (vmem,),
         scratch_shapes=[
             pltpu.VMEM((2, cols, tokens), BF16),
             pltpu.VMEM((2, cols, tokens), BF16),
@@ -493,41 +471,39 @@
             pltpu.VMEM((2, cols, lat), BF16),
             pltpu.VMEM((3, tokens, wide), BF16),
             pltpu.VMEM((3, half, wide), BF16),
-            pltpu.VMEM((3, 3, quarter, lat), BF16),
-            pltpu.VMEM((3, 3, quarter, lat + 128), BF16),
-            pltpu.VMEM((3, quarter, lat), BF16),
-            pltpu.VMEM((3, quarter, lat + 128), BF16),
+            pltpu.VMEM((3, Y - 1, quarter, wide), BF16),
             pltpu.VMEM((3, quarter, wide), BF16),
             pltpu.VMEM((3, own, wide), BF16),
-            pltpu.VMEM((4, tokens, wide), BF16),
+            pltpu.VMEM((4, tokens, 3 * lat), BF16),
             pltpu.VMEM((2, cols, tokens), BF16),
+            pltpu.VMEM((cols, tokens), BF16),
             pltpu.VMEM((cols, tokens), BF16),
             pltpu.VMEM((cols, tokens), BF16),
             pltpu.VMEM((8, cols), F32),
             pltpu.VMEM((8, cols), F32),
             pltpu.VMEM((4, cols, tokens), BF16),
             pltpu.VMEM((cols, lat), F32),
-            pltpu.VMEM((cols, lat), F32),
+            pltpu.VMEM((cols, lat), BF16),
+            pltpu.VMEM((cols, lat), BF16),
             dma((7,)),
             dma((3,)),
             dma((3,)),
-            dma((3, 3)),
-            dma((3, 3)),
-            dma((3, 3)),
-            dma((3, 3)),
+            dma((3, Y - 1)),
+            dma((3, Y - 1)),
             dma((3,)),
             dma((3,)),
             dma((4,)),
             dma((4,)),
+            dma((4, Y - 1)),
+            dma((4, Y - 1)),
             dma((4, Y)),
             dma((4, Y)),
-            dma((4, Y)),
-            dma((4, Y)),
-            dma((4,)),
-            dma((4,)),
+            dma((5,)),
+            dma((5,)),
             dma((4,)),
             dma((4,)),
             dma((2,)),
+            dma((3,)),
         ],
         compiler_params=pltpu.CompilerParams(
             collective_id=0, has_side_effects=True, vmem_limit_bytes=56 * 1024 * 1024

time: 81.9 us -> 72.9 us (0.89)
  the two profiles are of different devices: /device:TPU:73 before, /device:TPU:3 now
where the time goes in v3:
time: 72.9 us; the launch traced here: 72.7 us
  Pallas kernels  72 us (99%)
    pallas_call x1, Pallas kernels, per_device(): pl.pallas_call(functools.partial(kernel, n_pipe), out_shape=(jax.ShapeDty...  69.7 us
    pallas_call x1, Pallas kernels, per_device(): pl.pallas_call(place, out_shape=tuple((jax.ShapeDtypeStruct(array.shape,...  2.33 us

profile of v3, /device:TPU:3, one launch (start us, length us, event | category | flops | bytes accessed | tf_op | source)
XLA Modules:
  0.0 72.7 jit_solution(5571396192073735627)
XLA Ops:
  0.6 69.7 %shard_map.101 = (bf16[2,448,256]{2,1,0:T(8,128)(2,1)}, bf16[2,448,256]{2,1,0:T(8,128)(2,1)}, bf16[448,512]{1,0:T(8,128)(2,1)}, bf16[448,512]{1,0:T(8,128)(2,1)}, bf16[1,448]{1,0:T(2,128)(2,1)}) custom-call(bf16[2,448,256]{2,1,0:T(8,128)(2,1)} %bitcast.26, bf16[2,448,256]{2,1,0:T(8,128)(2,1)} %bitcast.27, bf16[2,448,256]{2,1,0:T(8,128)(2,1)} %bitcast.28, ...), custom_call_target="tpu_custom_call" | custom-call | tf_op jit(solution)/shard_map/pallas_call | solution.py:455
  70.3 2.3 %shard_map.102 = (bf16[2,448,256]{2,1,0:T(8,128)(2,1)}, bf16[2,448,256]{2,1,0:T(8,128)(2,1)}, bf16[448,512]{1,0:T(8,128)(2,1)}, bf16[448,512]{1,0:T(8,128)(2,1)}, bf16[1,448]{1,0:T(2,128)(2,1)}) custom-call(bf16[2,448,256]{2,1,0:T(8,128)(2,1)} %get-tuple-element.15.refs_0_, bf16[2,448,256]{2,1,0:T(8,128)(2,1)} %get-tuple-element.16.refs_1_, ...), custom_call_target="tpu_custom_call" | custom-call | tf_op jit(solution)/shard_map/pallas_call | solution.py:512

commit v4 on v3

--- a/solution.py
+++ b/solution.py
@@ -427,20 +427,15 @@
 
 
 def place(*refs):
-    count = (len(refs) - 2) // 3
-    sources, targets, held = refs[:count], refs[count : 2 * count], refs[2 * count : 3 * count]
-    arrive, leave = refs[3 * count :]
-    copies = []
-    for index in range(count):
-        first = pltpu.make_async_copy(sources[index], held[index], arrive.at[index])
-        second = pltpu.make_async_copy(held[index], targets[index], leave.at[index])
-        first.start()
-        copies.append((first, second))
-    for first, second in copies:
-        first.wait()
-        second.start()
-    for first, second in copies:
-        second.wait()
+    count = len(refs) // 2
+    sources, targets, sems = refs[:count], refs[count:-1], refs[-1]
+    copies = [
+        pltpu.make_async_copy(sources[index], targets[index], sems.at[index]) for index in range(count)
+    ]
+    for copy in copies:
+        copy.start()
+    for copy in copies:
+        copy.wait()
 
 
 def per_device(n_pipe, fwd_in, stash, cot_in, w_down, w_up, gain):
@@ -506,16 +501,16 @@
             dma((3,)),
         ],
         compiler_params=pltpu.CompilerParams(
-            collective_id=0, has_side_effects=True, vmem_limit_bytes=56 * 1024 * 1024
+            collective_id=0, has_side_effects=True, vmem_limit_bytes=52 * 1024 * 1024
         ),
     )(turned(fwd_in), turned(stash), turned(cot_in), w_down[0], turned(w_up), gain[0])
     fwd_next, bwd_next, grad_down, grad_up, grad_gain = pl.pallas_call(
         place,
         out_shape=tuple(jax.ShapeDtypeStruct(array.shape, array.dtype) for array in outs),
-        in_specs=[anywhere] * 5,
+        in_specs=[vmem] * 5,
         out_specs=(anywhere,) * 5,
-        scratch_shapes=[pltpu.VMEM(array.shape, array.dtype) for array in outs] + [dma((5,)), dma((5,))],
-        compiler_params=pltpu.CompilerParams(vmem_limit_bytes=56 * 1024 * 1024),
+        scratch_shapes=[dma((5,))],
+        compiler_params=pltpu.CompilerParams(vmem_limit_bytes=16 * 1024 * 1024),
     )(*outs)
     return (
         jnp.swapaxes(fwd_next, 1, 2)[None],

time: 72.9 us -> 71.2 us (0.977)
  Pallas kernels: 72 us -> 69.7 us
    pallas_call x1, Pallas kernels: 69.7 us -> 68.4 us  [per_device(): pl.pallas_call(functools.partial(kernel, n_pipe), out_shape=(jax.ShapeDty...]
    pallas_call x1, Pallas kernels: 2.33 us -> 1.27 us  [per_device(): pl.pallas_call(place, out_shape=tuple((jax.ShapeDtypeStruct(array.shape,...]
where the time goes in v4:
time: 71.2 us; the launch traced here: 71 us
  Pallas kernels  69.7 us (98%)
    pallas_call x1, Pallas kernels, per_device(): pl.pallas_call(functools.partial(kernel, n_pipe), out_shape=(jax.ShapeDty...  68.4 us

profile of v4, /device:TPU:3, one launch (start us, length us, event | category | flops | bytes accessed | tf_op | source)
XLA Modules:
  0.0 71.0 jit_solution(8131543320820768465)
XLA Ops:
  0.6 0.0 copy-start
  0.6 0.7 copy-done
  1.3 68.4 %shard_map.101 = (bf16[2,448,256]{2,1,0:T(8,128)(2,1)S(1)}, bf16[2,448,256]{2,1,0:T(8,128)(2,1)S(1)}, bf16[448,512]{1,0:T(8,128)(2,1)S(1)}, bf16[448,512]{1,0:T(8,128)(2,1)S(1)}, bf16[1,448]{1,0:T(2,128)(2,1)S(1)}) custom-call(bf16[2,448,256]{2,1,0:T(8,128)(2,1)} %bitcast.27, bf16[2,448,256]{2,1,0:T(8,128)(2,1)} %bitcast.28, bf16[2,448,256]{2,1,0:T(8,128)(2,1)} %bitcast.29, ...), custom_call_target="tpu_custom_call" | custom-call | tf_op jit(solution)/shard_map/pallas_call | solution.py:450
  69.7 1.3 %shard_map.102 = (bf16[2,448,256]{2,1,0:T(8,128)(2,1)}, bf16[2,448,256]{2,1,0:T(8,128)(2,1)}, bf16[448,512]{1,0:T(8,128)(2,1)}, bf16[448,512]{1,0:T(8,128)(2,1)}, bf16[1,448]{1,0:T(2,128)(2,1)}) custom-call(bf16[2,448,256]{2,1,0:T(8,128)(2,1)S(1)} %get-tuple-element.15.refs_0_, bf16[2,448,256]{2,1,0:T(8,128)(2,1)S(1)} %get-tuple-element.16.refs_1_, ...), custom_call_target="tpu_custom_call" | custom-call | tf_op jit(solution)/shard_map/pallas_call | solution.py:507
Async XLA Ops:
  0.6 0.7 copy-start

commit v5 on v4

--- a/solution.py
+++ b/solution.py
@@ -51,8 +51,6 @@
     grecv,
     rows_out,
     down_acc,
-    gd_held,
-    gu_held,
     in_sem,
     core_s,
     core_r,
@@ -71,7 +69,6 @@
     n_s,
     n_r,
     zero_sem,
-    w_sem,
 ):
     pos = lax.axis_index("pipe")
     d = lax.axis_index("dp")
@@ -371,16 +368,10 @@
     factor = tokens ** (-0.5)
     mirror_dy.wait_recv()
     up = dot(cot_ref[0], full[3, :, two : two + lat], 1, 0) + dot(md[...], full[3, :, :lat], 1, 0)
-    gu_held[...] = (up * factor).astype(BF16)
-    leaving = [pltpu.make_async_copy(gu_held, gu_out, w_sem.at[0])]
-    leaving[0].start()
+    gu_out[...] = (up * factor).astype(BF16)
     mirror_z.wait_recv()
-    for index in range(2):
-        rows = pl.ds(index * (cols // 2), cols // 2)
-        down = down_acc[rows, :] + dot(mz[rows, :], full[3, :, lat:two], 1, 0)
-        gd_held[rows, :] = (down * factor).astype(BF16)
-        leaving.append(pltpu.make_async_copy(gd_held.at[rows], gd_out.at[rows], w_sem.at[index + 1]))
-        leaving[-1].start()
+    down = down_acc[...] + dot(mz[...], full[3, :, lat:two], 1, 0)
+    gd_out[...] = (down * factor).astype(BF16)
     mirror_gain.wait_recv()
     gg_out[...] = ((gain_parts[0] + grecv[...])[0:1, :] * factor).astype(BF16)
 
@@ -398,8 +389,6 @@
     edge(pos == 0, fwd_out.at[0], bwd_out.at[1])
     edge(pos == n_pipe - 1, fwd_out.at[1], bwd_out.at[0])
 
-    for copy in leaving:
-        copy.wait()
     for index in range(4):
 
         @pl.when(ups[index % 2])
@@ -457,7 +446,7 @@
             jax.ShapeDtypeStruct((1, cols), BF16),
         ),
         in_specs=[anywhere] * 5 + [vmem],
-        out_specs=(anywhere,) * 4 + (vmem,),
+        out_specs=(anywhere, anywhere, vmem, vmem, vmem),
         scratch_shapes=[
             pltpu.VMEM((2, cols, tokens), BF16),
             pltpu.VMEM((2, cols, tokens), BF16),
@@ -478,8 +467,6 @@
             pltpu.VMEM((8, cols), F32),
             pltpu.VMEM((4, cols, tokens), BF16),
             pltpu.VMEM((cols, lat), F32),
-            pltpu.VMEM((cols, lat), BF16),
-            pltpu.VMEM((cols, lat), BF16),
             dma((7,)),
             dma((3,)),
             dma((3,)),
@@ -498,7 +485,6 @@
             dma((4,)),
             dma((4,)),
             dma((2,)),
-            dma((3,)),
         ],
         compiler_params=pltpu.CompilerParams(
             collective_id=0, has_side_effects=True, vmem_limit_bytes=52 * 1024 * 1024

time: 71.2 us -> 71.1 us (level)
  no operation moved by 1% of the time
where the time goes in v5:
time: 71.1 us; the launch traced here: 71 us
  Pallas kernels  69.6 us (98%)
    pallas_call x1, Pallas kernels, per_device(): pl.pallas_call(functools.partial(kernel, n_pipe), out_shape=(jax.ShapeDty...  68.4 us

profile of v5, /device:TPU:3, one launch (start us, length us, event | category | flops | bytes accessed | tf_op | source)
XLA Modules:
  0.0 71.0 jit_solution(7083583288561030861)
XLA Ops:
  0.6 0.0 copy-start
  0.6 0.7 copy-done
  1.3 68.4 %shard_map.101 = (bf16[2,448,256]{2,1,0:T(8,128)(2,1)S(1)}, bf16[2,448,256]{2,1,0:T(8,128)(2,1)S(1)}, bf16[448,512]{1,0:T(8,128)(2,1)S(1)}, bf16[448,512]{1,0:T(8,128)(2,1)S(1)}, bf16[1,448]{1,0:T(2,128)(2,1)S(1)}) custom-call(bf16[2,448,256]{2,1,0:T(8,128)(2,1)} %bitcast.27, bf16[2,448,256]{2,1,0:T(8,128)(2,1)} %bitcast.28, bf16[2,448,256]{2,1,0:T(8,128)(2,1)} %bitcast.29, ...), custom_call_target="tpu_custom_call" | custom-call | tf_op jit(solution)/shard_map/pallas_call | solution.py:439
  69.7 1.3 %shard_map.102 = (bf16[2,448,256]{2,1,0:T(8,128)(2,1)}, bf16[2,448,256]{2,1,0:T(8,128)(2,1)}, bf16[448,512]{1,0:T(8,128)(2,1)}, bf16[448,512]{1,0:T(8,128)(2,1)}, bf16[1,448]{1,0:T(2,128)(2,1)}) custom-call(bf16[2,448,256]{2,1,0:T(8,128)(2,1)S(1)} %get-tuple-element.15.refs_0_, bf16[2,448,256]{2,1,0:T(8,128)(2,1)S(1)} %get-tuple-element.16.refs_1_, ...), custom_call_target="tpu_custom_call" | custom-call | tf_op jit(solution)/shard_map/pallas_call | solution.py:493
Async XLA Ops:
  0.6 0.7 copy-start
